TPU v7x, 32 devices: a whole 2x2x4 slice. The times are simulated.
32 devices in a mesh: seq: 2 (over x), fsdp: 16 (over z, y, core).
Axes of the slice: x: 2, y: 2, z: 4, core: 2. Of those that a mesh axis runs over, the one named last changes fastest.
Arguments:
- tokens: bfloat16 [16, 256, 2048], P('fsdp', 'seq'), may hold values from -6 to 6
- norm_gain: bfloat16 [2048], P(('seq', 'fsdp')), may hold values from 0.5 to 1.5
- query_proj: bfloat16 [2048, 3072], P(('seq', 'fsdp')), may hold values from -0.125 to 0.125
- latent_proj: bfloat16 [2048, 576], P(('seq', 'fsdp')), may hold values from -0.125 to 0.125
- latent_gain: bfloat16 [512], P(('seq', 'fsdp')), may hold values from 0.5 to 1.5
- expand_proj: bfloat16 [512, 4096], P(('seq', 'fsdp')), may hold values from -0.25 to 0.25
- output_proj: bfloat16 [2048, 2048], P(('seq', 'fsdp')), may hold values from -0.5 to 0.5
- mixer_gain: bfloat16 [2048], P(('seq', 'fsdp')), may hold values from 0.5 to 1.5
- shared_gate: bfloat16 [2048, 2816], P(('seq', 'fsdp')), may hold values from -0.125 to 0.125
- shared_up: bfloat16 [2048, 2816], P(('seq', 'fsdp')), may hold values from -0.125 to 0.125
- shared_down: bfloat16 [2816, 2048], P(('seq', 'fsdp')), may hold values from -0.15625 to 0.15625
- expert_gate: bfloat16 [16, 2048, 1408], P('fsdp', None, 'seq'), may hold values from -0.125 to 0.125
- expert_up: bfloat16 [16, 2048, 1408], P('fsdp', None, 'seq'), may hold values from -0.125 to 0.125
- expert_down: bfloat16 [16, 1408, 2048], P('fsdp', 'seq'), may hold values from -0.4375 to 0.4375
- doc_starts: int32 [16, 256], P('fsdp'), may hold values from 0 to 1, as said below
- routes: int32 [16, 256, 6], P('fsdp', 'seq'), may hold values from 0 to 15, all different within a row; in each aligned block of 128 rows (0 to 127, 128 to 255, ..., all dimensions but the last counted through in order) at most 72 rows name the same one
- gate_levels: int32 [16, 256, 6], P('fsdp', 'seq'), may hold values from 1 to 8
- cotangent: bfloat16 [16, 256, 2048], P('fsdp', 'seq'), may hold values from -6 to 6
Outputs:
- layer_out: float32 [16, 256, 2048], P('fsdp', 'seq')
- input_grad: float32 [16, 256, 2048], P('fsdp', 'seq')
- norm_gain_grad: float32 [2048], P(('seq', 'fsdp'))
- query_proj_grad: float32 [2048, 3072], P(('seq', 'fsdp'))
- latent_proj_grad: float32 [2048, 576], P(('seq', 'fsdp'))
- latent_gain_grad: float32 [512], P(('seq', 'fsdp'))
- expand_proj_grad: float32 [512, 4096], P(('seq', 'fsdp'))
- output_proj_grad: float32 [2048, 2048], P(('seq', 'fsdp'))
- mixer_gain_grad: float32 [2048], P(('seq', 'fsdp'))
- shared_gate_grad: float32 [2048, 2816], P(('seq', 'fsdp'))
- shared_up_grad: float32 [2048, 2816], P(('seq', 'fsdp'))
- shared_down_grad: float32 [2816, 2048], P(('seq', 'fsdp'))
- expert_gate_grad: float32 [16, 2048, 1408], P('fsdp', None, 'seq')
- expert_up_grad: float32 [16, 2048, 1408], P('fsdp', None, 'seq')
- expert_down_grad: float32 [16, 1408, 2048], P('fsdp', 'seq')
Inputs may be any that keep to these rules, and one draw needn't show every extreme that they name: `doc_starts`: every sequence starts a document at position 0 and has at most one more start, after position 160. `routes`: A token names 6 different experts; among the 128 rows of one device no expert is named more than 72 times, a bound that some block reaches.
All inputs are finite; a program needn't handle non-finite values.
Results may differ from a plain program's by a relative error of at most 0.018.
Values may be sent and summed in bfloat16 or wider, within the bound.
A program may use at most 384 MiB of HBM per device.

v0:
```python
import jax
import jax.numpy as jnp
from jax import lax
from jax.sharding import PartitionSpec as P

H = 16
DN = 128
DR = 64
DV = 128
KVL = 512
TOPK = 6


norm_epsilon = 1e-06
rotary_base = 10000.0


def norm_apply(values, gain):
    inverse = lax.rsqrt(jnp.mean(values * values, axis=-1, keepdims=True) + norm_epsilon)
    return values * inverse * gain


def sigmoid_linear(values):
    return values * jax.nn.sigmoid(values)


def rotary_tables(positions, width):
    halfway = width // 2
    frequency = rotary_base ** (-2.0 * jnp.arange(halfway, dtype=jnp.float32) / width)
    angles = positions.astype(jnp.float32)[:, None] * frequency[None, :]
    return (jnp.cos(angles), jnp.sin(angles))


def rotate(values, cosine, sine):
    halfway = values.shape[-1] // 2
    leading = values[..., :halfway]
    trailing = values[..., halfway:]
    return jnp.concatenate(
        [leading * cosine - trailing * sine, leading * sine + trailing * cosine], axis=-1
    )


def contract(left, right, left_dim, right_dim):
    return lax.dot_general(
        left, right, (((left_dim,), (right_dim,)), ((), ())), preferred_element_type=jnp.float32
    )


def silu_slope(values):
    sigma = jax.nn.sigmoid(values)
    return sigma * (1.0 + values * (1.0 - sigma))


def forward(params, tokens, doc_starts, routes, gate_levels):
    (
        norm_gain,
        query_proj,
        latent_proj,
        latent_gain,
        expand_proj,
        output_proj,
        mixer_gain,
        shared_gate,
        shared_up,
        shared_down,
        expert_gate,
        expert_up,
        expert_down,
    ) = params
    gathered = (
        lax.all_gather(norm_gain, ("seq", "fsdp"), axis=0, tiled=True),
        lax.all_gather(query_proj, ("seq", "fsdp"), axis=0, tiled=True),
        lax.all_gather(latent_proj, ("seq", "fsdp"), axis=0, tiled=True),
        lax.all_gather(latent_gain, ("seq", "fsdp"), axis=0, tiled=True),
        lax.all_gather(expand_proj, ("seq", "fsdp"), axis=0, tiled=True),
        lax.all_gather(output_proj, ("seq", "fsdp"), axis=0, tiled=True),
        lax.all_gather(mixer_gain, ("seq", "fsdp"), axis=0, tiled=True),
        lax.all_gather(shared_gate, ("seq", "fsdp"), axis=0, tiled=True),
        lax.all_gather(shared_up, ("seq", "fsdp"), axis=0, tiled=True),
        lax.all_gather(shared_down, ("seq", "fsdp"), axis=0, tiled=True),
    )
    inputs = tokens[0].astype(jnp.float32)
    tok_count = inputs.shape[0]
    normed = norm_apply(inputs, gathered[0].astype(jnp.float32)).astype(jnp.bfloat16)
    query_raw = jnp.dot(normed, gathered[1], preferred_element_type=jnp.float32).reshape(
        tok_count, H, DN + DR
    )
    latent_raw = jnp.dot(normed, gathered[2], preferred_element_type=jnp.float32)
    latent = latent_raw[:, :KVL]
    latent_normed = norm_apply(latent, gathered[3].astype(jnp.float32)).astype(jnp.bfloat16)
    expanded = jnp.dot(latent_normed, gathered[4], preferred_element_type=jnp.float32).reshape(
        tok_count, H, DN + DV
    )
    positions = lax.axis_index("seq") * tok_count + jnp.arange(tok_count, dtype=jnp.int32)
    cosine, sine = rotary_tables(positions, DR)
    query = jnp.concatenate(
        [query_raw[:, :, :DN], rotate(query_raw[:, :, DN:], cosine[:, None, :], sine[:, None, :])],
        axis=2,
    ).astype(jnp.bfloat16)
    key_rotary = rotate(latent_raw[:, KVL:], cosine, sine)
    keys = jnp.concatenate(
        [expanded[:, :, :DN], jnp.broadcast_to(key_rotary[:, None, :], (tok_count, H, DR))], axis=2
    ).astype(jnp.bfloat16)
    values = expanded[:, :, DN:].astype(jnp.bfloat16)
    head_query, head_keys, head_values = (
        lax.all_to_all(query, "seq", split_axis=1, concat_axis=0, tiled=True),
        lax.all_to_all(keys, "seq", split_axis=1, concat_axis=0, tiled=True),
        lax.all_to_all(values, "seq", split_axis=1, concat_axis=0, tiled=True),
    )
    documents = jnp.cumsum(doc_starts[0])
    spots = jnp.arange(documents.shape[0])
    allowed = (spots[None, :] <= spots[:, None]) & (documents[None, :] == documents[:, None])
    scores = jnp.einsum(
        "qhd,khd->hqk", head_query, head_keys, preferred_element_type=jnp.float32
    ) * (DN + DR) ** (-0.5)
    scores = jnp.where(allowed[None], scores, -1e30)
    raised = jnp.exp(scores - jnp.max(scores, axis=-1, keepdims=True))
    soft = raised / jnp.sum(raised, axis=-1, keepdims=True)
    soft_low = soft.astype(jnp.bfloat16)
    mixed = jnp.einsum(
        "hqk,khd->qhd", soft_low, head_values, preferred_element_type=jnp.float32
    ).astype(jnp.bfloat16)
    returned = lax.all_to_all(mixed, "seq", split_axis=0, concat_axis=1, tiled=True)
    attended = returned.reshape(tok_count, H * DV)
    middle = inputs + jnp.dot(attended, gathered[5], preferred_element_type=jnp.float32)
    normed_two = norm_apply(middle, gathered[6].astype(jnp.float32)).astype(jnp.bfloat16)
    shared_pre = jnp.dot(normed_two, gathered[7], preferred_element_type=jnp.float32)
    shared_lift = jnp.dot(normed_two, gathered[8], preferred_element_type=jnp.float32)
    shared_hidden = (sigmoid_linear(shared_pre) * shared_lift).astype(jnp.bfloat16)
    shared_result = jnp.dot(shared_hidden, gathered[9], preferred_element_type=jnp.float32)
    experts_count = lax.axis_size("fsdp")
    capacity = max(2, 3 * tok_count * TOPK // (2 * experts_count))
    chosen = routes[0].reshape(-1)
    matches = (chosen[:, None] == jnp.arange(experts_count, dtype=jnp.int32)[None, :]).astype(
        jnp.int32
    )
    earlier = jnp.sum((jnp.cumsum(matches, axis=0) - matches) * matches, axis=1)
    slots = chosen * capacity + earlier
    filled = (
        jnp.zeros((experts_count * capacity,), jnp.int32)
        .at[slots]
        .set(jnp.arange(chosen.shape[0], dtype=jnp.int32) + 1)
    )
    present = filled > 0
    sources = jnp.maximum(filled - 1, 0)
    outgoing = jnp.where(
        present[:, None], jnp.take(normed_two, sources // TOPK, axis=0), jnp.zeros((), jnp.bfloat16)
    )
    arrived = lax.all_to_all(
        outgoing.reshape(experts_count, capacity, -1),
        "fsdp",
        split_axis=0,
        concat_axis=0,
        tiled=True,
    )
    paired = lax.all_gather(arrived, "seq", axis=0, tiled=True)
    expert_rows = paired.reshape(-1, paired.shape[-1])
    gate_weight, up_weight, down_weight = (expert_gate[0], expert_up[0], expert_down[0])
    expert_pre = jnp.dot(expert_rows, gate_weight, preferred_element_type=jnp.float32)
    expert_lift = jnp.dot(expert_rows, up_weight, preferred_element_type=jnp.float32)
    expert_hidden = (sigmoid_linear(expert_pre) * expert_lift).astype(jnp.bfloat16)
    partial_out = jnp.dot(expert_hidden, down_weight, preferred_element_type=jnp.float32)
    summed = lax.psum_scatter(
        partial_out.reshape(paired.shape).astype(jnp.bfloat16),
        "seq",
        scatter_dimension=0,
        tiled=True,
    )
    results = lax.all_to_all(summed, "fsdp", split_axis=0, concat_axis=0, tiled=True)
    picked = jnp.take(results.reshape(experts_count * capacity, -1), slots, axis=0)
    picked = picked.astype(jnp.float32).reshape(tok_count, TOPK, -1)
    levels = gate_levels[0].astype(jnp.float32)
    gate_share = levels / jnp.sum(levels, axis=1, keepdims=True)
    routed = jnp.sum(gate_share[:, :, None] * picked, axis=1)
    output = middle + shared_result + routed
    return dict(
        gathered=gathered,
        inputs=inputs,
        normed=normed,
        latent=latent,
        latent_normed=latent_normed,
        cosine=cosine,
        sine=sine,
        head_query=head_query,
        head_keys=head_keys,
        head_values=head_values,
        soft=soft,
        soft_low=soft_low,
        attended=attended,
        middle=middle,
        normed_two=normed_two,
        shared_pre=shared_pre,
        shared_lift=shared_lift,
        shared_hidden=shared_hidden,
        capacity=capacity,
        slots=slots,
        present=present,
        sources=sources,
        expert_rows=expert_rows,
        expert_pre=expert_pre,
        expert_lift=expert_lift,
        expert_hidden=expert_hidden,
        expert_weights=(gate_weight, up_weight, down_weight),
        gate_share=gate_share,
        output=output,
    )


def backward(saved, cotangent):
    gate_weight, up_weight, down_weight = saved["expert_weights"]
    gathered = saved["gathered"]
    grad_out = cotangent[0].astype(jnp.float32)
    grad_low = cotangent[0]
    tok_count = grad_out.shape[0]
    experts_count = lax.axis_size("fsdp")
    capacity = saved["capacity"]
    d_picked = (saved["gate_share"][:, :, None] * grad_out[:, None, :]).astype(jnp.bfloat16)
    d_picked = d_picked.reshape(tok_count * TOPK, -1)
    d_slots = jnp.where(
        saved["present"][:, None],
        jnp.take(d_picked, saved["sources"], axis=0),
        jnp.zeros((), jnp.bfloat16),
    )
    d_arrived = lax.all_to_all(
        d_slots.reshape(experts_count, capacity, -1),
        "fsdp",
        split_axis=0,
        concat_axis=0,
        tiled=True,
    )
    d_paired = lax.all_gather(d_arrived, "seq", axis=0, tiled=True)
    d_expert_out = d_paired.reshape(-1, d_paired.shape[-1])
    expert_pre = saved["expert_pre"]
    expert_rows = saved["expert_rows"]
    expert_down_grad = contract(saved["expert_hidden"], d_expert_out, 0, 0)
    d_hidden = contract(d_expert_out, down_weight, 1, 1)
    d_pre = (d_hidden * saved["expert_lift"] * silu_slope(expert_pre)).astype(jnp.bfloat16)
    d_lift = (d_hidden * sigmoid_linear(expert_pre)).astype(jnp.bfloat16)
    expert_gate_grad = contract(expert_rows, d_pre, 0, 0)
    expert_up_grad = contract(expert_rows, d_lift, 0, 0)
    d_rows = contract(d_pre, gate_weight, 1, 1) + contract(d_lift, up_weight, 1, 1)
    d_summed = lax.psum_scatter(
        d_rows.reshape(d_paired.shape).astype(jnp.bfloat16), "seq", scatter_dimension=0, tiled=True
    )
    d_back = lax.all_to_all(d_summed, "fsdp", split_axis=0, concat_axis=0, tiled=True)
    d_routed = jnp.take(d_back.reshape(experts_count * capacity, -1), saved["slots"], axis=0)
    d_routed = jnp.sum(d_routed.astype(jnp.float32).reshape(tok_count, TOPK, -1), axis=1)
    shared_pre = saved["shared_pre"]
    normed_two = saved["normed_two"]
    shared_down_grad = contract(saved["shared_hidden"], grad_low, 0, 0)
    d_shared_hidden = contract(grad_low, gathered[9], 1, 1)
    d_shared_pre = (d_shared_hidden * saved["shared_lift"] * silu_slope(shared_pre)).astype(
        jnp.bfloat16
    )
    d_shared_lift = (d_shared_hidden * sigmoid_linear(shared_pre)).astype(jnp.bfloat16)
    shared_gate_grad = contract(normed_two, d_shared_pre, 0, 0)
    shared_up_grad = contract(normed_two, d_shared_lift, 0, 0)
    d_normed_two = (
        contract(d_shared_pre, gathered[7], 1, 1)
        + contract(d_shared_lift, gathered[8], 1, 1)
        + d_routed
    )
    mixer_value, mixer_pull = jax.vjp(norm_apply, saved["middle"], gathered[6].astype(jnp.float32))
    d_middle_norm, mixer_gain_grad = mixer_pull(d_normed_two)
    d_middle = grad_out + d_middle_norm
    d_attn = d_middle.astype(jnp.bfloat16)
    output_proj_grad = contract(saved["attended"], d_attn, 0, 0)
    d_attended = contract(d_attn, gathered[5], 1, 1).astype(jnp.bfloat16).reshape(tok_count, H, DV)
    d_mixed = lax.all_to_all(d_attended, "seq", split_axis=1, concat_axis=0, tiled=True)
    soft = saved["soft"]
    d_soft = jnp.einsum(
        "qhd,khd->hqk", d_mixed, saved["head_values"], preferred_element_type=jnp.float32
    )
    delta = jnp.sum(soft * d_soft, axis=-1, keepdims=True)
    d_scores = (soft * (d_soft - delta)).astype(jnp.bfloat16)
    score_scale = (DN + DR) ** (-0.5)
    d_head_values = jnp.einsum(
        "hqk,qhd->khd", saved["soft_low"], d_mixed, preferred_element_type=jnp.float32
    ).astype(jnp.bfloat16)
    d_head_query = (
        jnp.einsum("hqk,khd->qhd", d_scores, saved["head_keys"], preferred_element_type=jnp.float32)
        * score_scale
    ).astype(jnp.bfloat16)
    d_head_keys = (
        jnp.einsum(
            "hqk,qhd->khd", d_scores, saved["head_query"], preferred_element_type=jnp.float32
        )
        * score_scale
    ).astype(jnp.bfloat16)
    d_query, d_keys, d_values = (
        lax.all_to_all(d_head_query, "seq", split_axis=0, concat_axis=1, tiled=True),
        lax.all_to_all(d_head_keys, "seq", split_axis=0, concat_axis=1, tiled=True),
        lax.all_to_all(d_head_values, "seq", split_axis=0, concat_axis=1, tiled=True),
    )
    cosine = saved["cosine"]
    sine = saved["sine"]
    normed = saved["normed"]
    d_query_float = d_query.astype(jnp.float32)
    d_query_raw = (
        jnp.concatenate(
            [
                d_query_float[:, :, :DN],
                rotate(d_query_float[:, :, DN:], cosine[:, None, :], -sine[:, None, :]),
            ],
            axis=2,
        )
        .astype(jnp.bfloat16)
        .reshape(tok_count, -1)
    )
    query_proj_grad = contract(normed, d_query_raw, 0, 0)
    d_key_rotary = rotate(jnp.sum(d_keys[:, :, DN:].astype(jnp.float32), axis=1), cosine, -sine)
    d_expanded = jnp.concatenate([d_keys[:, :, :DN], d_values], axis=2).reshape(tok_count, -1)
    expand_proj_grad = contract(saved["latent_normed"], d_expanded, 0, 0)
    d_latent_normed = contract(d_expanded, gathered[4], 1, 1)
    latent_value, latent_pull = jax.vjp(
        norm_apply, saved["latent"], gathered[3].astype(jnp.float32)
    )
    d_latent, latent_gain_grad = latent_pull(d_latent_normed)
    d_latent_raw = jnp.concatenate([d_latent, d_key_rotary], axis=1).astype(jnp.bfloat16)
    latent_proj_grad = contract(normed, d_latent_raw, 0, 0)
    d_normed = contract(d_query_raw, gathered[1], 1, 1) + contract(d_latent_raw, gathered[2], 1, 1)
    input_value, input_pull = jax.vjp(norm_apply, saved["inputs"], gathered[0].astype(jnp.float32))
    d_inputs, norm_gain_grad = input_pull(d_normed)
    input_grad = d_middle + d_inputs
    reduced = (
        lax.psum_scatter(norm_gain_grad, ("seq", "fsdp"), scatter_dimension=0, tiled=True),
        lax.psum_scatter(query_proj_grad, ("seq", "fsdp"), scatter_dimension=0, tiled=True),
        lax.psum_scatter(latent_proj_grad, ("seq", "fsdp"), scatter_dimension=0, tiled=True),
        lax.psum_scatter(latent_gain_grad, ("seq", "fsdp"), scatter_dimension=0, tiled=True),
        lax.psum_scatter(expand_proj_grad, ("seq", "fsdp"), scatter_dimension=0, tiled=True),
        lax.psum_scatter(output_proj_grad, ("seq", "fsdp"), scatter_dimension=0, tiled=True),
        lax.psum_scatter(mixer_gain_grad, ("seq", "fsdp"), scatter_dimension=0, tiled=True),
        lax.psum_scatter(shared_gate_grad, ("seq", "fsdp"), scatter_dimension=0, tiled=True),
        lax.psum_scatter(shared_up_grad, ("seq", "fsdp"), scatter_dimension=0, tiled=True),
        lax.psum_scatter(shared_down_grad, ("seq", "fsdp"), scatter_dimension=0, tiled=True),
    )
    return (input_grad, reduced, expert_gate_grad, expert_up_grad, expert_down_grad)


def body(
    tokens,
    norm_gain,
    query_proj,
    latent_proj,
    latent_gain,
    expand_proj,
    output_proj,
    mixer_gain,
    shared_gate,
    shared_up,
    shared_down,
    expert_gate,
    expert_up,
    expert_down,
    doc_starts,
    routes,
    gate_levels,
    cotangent,
):
    params = (
        norm_gain,
        query_proj,
        latent_proj,
        latent_gain,
        expand_proj,
        output_proj,
        mixer_gain,
        shared_gate,
        shared_up,
        shared_down,
        expert_gate,
        expert_up,
        expert_down,
    )
    saved = forward(params, tokens, doc_starts, routes, gate_levels)
    layer_out = saved["output"]
    barrier = lax.optimization_barrier((params, layer_out))
    saved = forward(barrier[0], tokens, doc_starts, routes, gate_levels)
    input_grad, reduced, expert_gate_grad, expert_up_grad, expert_down_grad = backward(
        saved, cotangent
    )
    return (
        layer_out[None],
        input_grad[None],
        reduced[0],
        reduced[1],
        reduced[2],
        reduced[3],
        reduced[4],
        reduced[5],
        reduced[6],
        reduced[7],
        reduced[8],
        reduced[9],
        expert_gate_grad[None],
        expert_up_grad[None],
        expert_down_grad[None],
    )


def solution(mesh):
    in_specs = (
        P("fsdp", "seq", None),
        P(("seq", "fsdp")),
        P(("seq", "fsdp"), None),
        P(("seq", "fsdp"), None),
        P(("seq", "fsdp")),
        P(("seq", "fsdp"), None),
        P(("seq", "fsdp"), None),
        P(("seq", "fsdp")),
        P(("seq", "fsdp"), None),
        P(("seq", "fsdp"), None),
        P(("seq", "fsdp"), None),
        P("fsdp", None, "seq"),
        P("fsdp", None, "seq"),
        P("fsdp", "seq", None),
        P("fsdp", None),
        P("fsdp", "seq", None),
        P("fsdp", "seq", None),
        P("fsdp", "seq", None),
    )
    out_specs = (
        P("fsdp", "seq", None),
        P("fsdp", "seq", None),
        P(("seq", "fsdp")),
        P(("seq", "fsdp"), None),
        P(("seq", "fsdp"), None),
        P(("seq", "fsdp")),
        P(("seq", "fsdp"), None),
        P(("seq", "fsdp"), None),
        P(("seq", "fsdp")),
        P(("seq", "fsdp"), None),
        P(("seq", "fsdp"), None),
        P(("seq", "fsdp"), None),
        P("fsdp", None, "seq"),
        P("fsdp", None, "seq"),
        P("fsdp", "seq", None),
    )
    return jax.shard_map(body, mesh=mesh, in_specs=in_specs, out_specs=out_specs, check_vma=False)
```

profile of v0, /device:TPU:0, one launch (start us, length us, event | category | flops | bytes accessed | tf_op | source)
XLA Modules:
  0.0 3695.2 jit_solution(9362682793183307086)
XLA Ops:
  14.7 42.3 %all-reduce.11 = (bf16[2048]{0:T(1024)(128)(2,1)S(1)}, bf16[512]{0:T(512)(128)(2,1)S(1)}, bf16[2048]{0:T(1024)(128)(2,1)S(1)}) all-reduce(bf16[2048]{0:T(1024)(128)(2,1)S(1)} %dynamic-update-slice, bf16[512]{0:T(512)(128)(2,1)S(1)} %dynamic-update-slice.1, ...), channel_id=1, replica_groups=mesh['seq'=2,'fsdp'=16] {'seq','fsdp'}, use_global_device_ids=true, to_apply=%add | all-reduce | flops 4608 | bytes 18432
  74.9 60.7 %all-gather.20.cloned.1.call-done = bf16[512,4096]{1,0:T(8,128)(2,1)} async-done(((bf16[16,4096]{1,0:T(8,128)(2,1)}), bf16[512,4096]{1,0:T(8,128)(2,1)}) %all-gather.20.cloned.1.call-update) | async-done | bytes 4194320 | tf_op jit(solution)/shard_map/all_gather | solution.py:75
  147.6 87.7 %all-gather.22.cloned.1.call-done = bf16[2048,3072]{1,0:T(8,128)(2,1)} async-done(((bf16[64,3072]{1,0:T(8,128)(2,1)}), bf16[2048,3072]{1,0:T(8,128)(2,1)}) %all-gather.22.cloned.1.call-update) | async-done | bytes 12582928 | tf_op jit(solution)/shard_map/all_gather | solution.py:72
  235.4 16.5 copy.133
  332.7 110.2 %all_to_all.226 = bf16[16,72,2048]{2,1,0:T(8,128)(2,1)} all-to-all(bf16[16,72,2048]{2,1,0:T(8,128)(2,1)S(1)} %bitcast.300), channel_id=1, replica_groups=mesh['seq'=2,'fsdp'=16] {'fsdp'}, dimensions={0} | all-to-all | bytes 9437184 | tf_op jit(solution)/shard_map/all_to_all | solution.py:149
  443.4 117.6 %all-gather.32.cloned.1.call-done = bf16[32,72,2048]{2,1,0:T(8,128)(2,1)} async-done(((bf16[16,72,2048]{2,1,0:T(8,128)(2,1)}), bf16[32,72,2048]{2,1,0:T(8,128)(2,1)}) %all-gather.32.cloned.1.call-update) | async-done | bytes 9437200 | tf_op jit(solution)/shard_map/all_gather | solution.py:156
  600.3 108.5 %reduce-scatter.10.cloned.1.call-done = bf16[16,72,2048]{2,1,0:T(8,128)(2,1)} async-done(((bf16[32,72,2048]{2,1,0:T(8,128)(2,1)}), bf16[16,72,2048]{2,1,0:T(8,128)(2,1)}) %reduce-scatter.10.cloned.1.call-update) | async-done | bytes 4718608 | tf_op jit(solution)/shard_map/reduce_scatter | solution.py:163
  714.9 161.2 %all-gather.26.cloned.1.call-done = bf16[2048,2816]{1,0:T(8,128)(2,1)} async-done(((bf16[64,2816]{1,0:T(8,128)(2,1)}), bf16[2048,2816]{1,0:T(8,128)(2,1)}) %all-gather.26.cloned.1.call-update) | async-done | bytes 11534352 | tf_op jit(solution)/shard_map/all_gather | solution.py:78
  913.8 54.5 %all-gather.28.cloned.1.call-done = bf16[2048,2816]{1,0:T(8,128)(2,1)} async-done(((bf16[64,2816]{1,0:T(8,128)(2,1)}), bf16[2048,2816]{1,0:T(8,128)(2,1)}) %all-gather.28.cloned.1.call-update) | async-done | bytes 11534352 | tf_op jit(solution)/shard_map/all_gather | solution.py:79
  968.3 92.5 %all-gather.30.cloned.1.call-done = bf16[2816,2048]{1,0:T(8,128)(2,1)} async-done(((bf16[88,2048]{1,0:T(8,128)(2,1)}), bf16[2816,2048]{1,0:T(8,128)(2,1)}) %all-gather.30.cloned.1.call-update) | async-done | bytes 11534352 | tf_op jit(solution)/shard_map/all_gather | solution.py:80
  1076.7 39.2 %all-reduce.10 = (bf16[2048]{0:T(1024)(128)(2,1)S(1)}, bf16[512]{0:T(512)(128)(2,1)S(1)}, bf16[2048]{0:T(1024)(128)(2,1)}) all-reduce(bf16[2048]{0:T(1024)(128)(2,1)S(1)} %dynamic-update-slice.3, bf16[512]{0:T(512)(128)(2,1)S(1)} %dynamic-update-slice.4, ...), channel_id=1, replica_groups=mesh['seq'=2,'fsdp'=16] {'seq','fsdp'}, use_global_device_ids=true, to_apply=%add.3 | all-reduce | flops 4608 | bytes 18432
  1115.8 14.5 all-gather.36.cloned.1.call-done
  1133.5 60.7 %all-gather.38.cloned.1.call-done = bf16[512,4096]{1,0:T(8,128)(2,1)} async-done(((bf16[16,4096]{1,0:T(8,128)(2,1)}), bf16[512,4096]{1,0:T(8,128)(2,1)}) %all-gather.38.cloned.1.call-update) | async-done | bytes 4194320 | tf_op jit(solution)/shard_map/all_gather | solution.py:75
  1206.3 87.6 %all-gather.40.cloned.1.call-done = bf16[2048,3072]{1,0:T(8,128)(2,1)} async-done(((bf16[64,3072]{1,0:T(8,128)(2,1)}), bf16[2048,3072]{1,0:T(8,128)(2,1)}) %all-gather.40.cloned.1.call-update) | async-done | bytes 12582928 | tf_op jit(solution)/shard_map/all_gather | solution.py:72
  1293.8 16.8 copy.149
  1432.5 54.4 %all-to-all-done.11 = bf16[16,72,2048]{2,1,0:T(8,128)(2,1)} async-done(((bf16[16,72,2048]{2,1,0:T(8,128)(2,1)}), bf16[16,72,2048]{2,1,0:T(8,128)(2,1)}, u32[]{:S(2)}, u32[]{:S(2)}) %all-to-all-start.11) | async-done | bytes 4718624 | tf_op jit(solution)/shard_map/all_to_all | solution.py:149
  1489.8 125.1 %all_to_all.227 = bf16[16,72,2048]{2,1,0:T(8,128)(2,1)} all-to-all(bf16[16,72,2048]{2,1,0:T(8,128)(2,1)S(1)} %select_select_fusion.2), channel_id=1, replica_groups=mesh['seq'=2,'fsdp'=16] {'fsdp'}, dimensions={0} | all-to-all | bytes 9437184 | tf_op jit(solution)/shard_map/all_to_all | solution.py:224
  1643.5 97.5 %all-gather.48.cloned.1.call-done = bf16[32,72,2048]{2,1,0:T(8,128)(2,1)} async-done(((bf16[16,72,2048]{2,1,0:T(8,128)(2,1)}), bf16[32,72,2048]{2,1,0:T(8,128)(2,1)}) %all-gather.48.cloned.1.call-update) | async-done | bytes 9437200 | tf_op jit(solution)/shard_map/all_gather | solution.py:231
  1740.9 14.5 multiply_convert_fusion.1
  1780.9 53.9 %all-gather.46.cloned.1.call-done = bf16[2048,2816]{1,0:T(8,128)(2,1)} async-done(((bf16[64,2816]{1,0:T(8,128)(2,1)}), bf16[2048,2816]{1,0:T(8,128)(2,1)}) %all-gather.46.cloned.1.call-update) | async-done | bytes 11534352 | tf_op jit(solution)/shard_map/all_gather | solution.py:78
  1840.8 86.4 %all-gather.44.cloned.1.call-done = bf16[2048,2816]{1,0:T(8,128)(2,1)} async-done(((bf16[64,2816]{1,0:T(8,128)(2,1)}), bf16[2048,2816]{1,0:T(8,128)(2,1)}) %all-gather.44.cloned.1.call-update) | async-done | bytes 11534352 | tf_op jit(solution)/shard_map/all_gather | solution.py:79
  1943.3 76.2 %all-gather.34.cloned.1.call-done = bf16[2816,2048]{1,0:T(8,128)(2,1)} async-done(((bf16[88,2048]{1,0:T(8,128)(2,1)}), bf16[2816,2048]{1,0:T(8,128)(2,1)}) %all-gather.34.cloned.1.call-update) | async-done | bytes 11534352 | tf_op jit(solution)/shard_map/all_gather | solution.py:80
  2050.0 80.7 %reduce-scatter.12.cloned.1.call-done = bf16[16,72,2048]{2,1,0:T(8,128)(2,1)} async-done(((bf16[32,72,2048]{2,1,0:T(8,128)(2,1)}), bf16[16,72,2048]{2,1,0:T(8,128)(2,1)}) %reduce-scatter.12.cloned.1.call-update) | async-done | bytes 4718608 | tf_op jit(solution)/shard_map/reduce_scatter | solution.py:242
  2145.0 113.7 %all-to-all-done.12 = bf16[16,72,2048]{2,1,0:T(8,128)(2,1)} async-done(((bf16[16,72,2048]{2,1,0:T(8,128)(2,1)}), bf16[16,72,2048]{2,1,0:T(8,128)(2,1)}, u32[]{:S(2)}, u32[]{:S(2)}) %all-to-all-start.12) | async-done | bytes 4718624 | tf_op jit(solution)/shard_map/all_to_all | solution.py:245
  2379.0 15.2 all_to_all.229
  2454.3 89.5 %all-reduce.9 = (f32[2048]{0:T(1024)S(1)}, f32[512]{0:T(512)S(1)}, f32[2048]{0:T(1024)S(1)}) all-reduce(f32[2048]{0:T(1024)} %get-tuple-element.45, f32[512]{0:T(512)} %get-tuple-element.47, f32[2048]{0:T(1024)} %get-tuple-element.43), channel_id=4, replica_groups=mesh['seq'=2,'fsdp'=16] {'seq','fsdp'}, use_global_device_ids=true, to_apply=%region_26.29.clone | all-reduce | flops 4608 | bytes 36864
  2549.1 154.9 %reduce-scatter.24.cloned.1.call-done = f32[64,2816]{1,0:T(8,128)} async-done(((f32[2048,2816]{1,0:T(8,128)}), f32[64,2816]{1,0:T(8,128)}) %reduce-scatter.24.cloned.1.call-update) | async-done | bytes 720912 | tf_op jit(solution)/shard_map/reduce_scatter | solution.py:334
  2704.0 251.9 %reduce-scatter.22.cloned.1.call-done = f32[64,2816]{1,0:T(8,128)} async-done(((f32[2048,2816]{1,0:T(8,128)}), f32[64,2816]{1,0:T(8,128)}) %reduce-scatter.22.cloned.1.call-update) | async-done | bytes 720912 | tf_op jit(solution)/shard_map/reduce_scatter | solution.py:333
  2955.9 148.2 %reduce-scatter.16.cloned.1.call-done = f32[64,576]{1,0:T(8,128)} async-done(((f32[2048,576]{1,0:T(8,128)}), f32[64,576]{1,0:T(8,128)}) %reduce-scatter.16.cloned.1.call-update) | async-done | bytes 147472 | tf_op jit(solution)/shard_map/reduce_scatter | solution.py:328
  3104.1 147.2 %reduce-scatter.18.cloned.1.call-done = f32[16,4096]{1,0:T(8,128)} async-done(((f32[512,4096]{1,0:T(8,128)}), f32[16,4096]{1,0:T(8,128)}) %reduce-scatter.18.cloned.1.call-update) | async-done | bytes 262160 | tf_op jit(solution)/shard_map/reduce_scatter | solution.py:330
  3251.4 183.5 %reduce-scatter.20.cloned.1.call-done = f32[64,2048]{1,0:T(8,128)} async-done(((f32[2048,2048]{1,0:T(8,128)}), f32[64,2048]{1,0:T(8,128)}) %reduce-scatter.20.cloned.1.call-update) | async-done | bytes 524304 | tf_op jit(solution)/shard_map/reduce_scatter | solution.py:331
  3434.9 253.2 %reduce-scatter.14.cloned.1.call-done = f32[64,3072]{1,0:T(8,128)} async-done(((f32[2048,3072]{1,0:T(8,128)}), f32[64,3072]{1,0:T(8,128)}) %reduce-scatter.14.cloned.1.call-update) | async-done | bytes 786448 | tf_op jit(solution)/shard_map/reduce_scatter | solution.py:327
  (432 shorter events, 662.6 us)
Async XLA Ops:
  7.2 64.5 %all-gather.18.cloned.1.call-start = ((), (), s32[]{:S(2)}) async-start(), calls=%async_computation.26 | async-start | bytes 2703360 | tf_op jit(solution)/shard_map/all_gather | solution.py:73
  7.9 127.6 %all-gather.20.cloned.1.call-start = ((), (), s32[]{:S(2)}) async-start(), calls=%async_computation.27 | async-start | bytes 4325376 | tf_op jit(solution)/shard_map/all_gather | solution.py:75
  8.7 226.7 %all-gather.22.cloned.1.call-start = ((), (), s32[]{:S(2)}) async-start(), calls=%async_computation.28 | async-start | bytes 12976128 | tf_op jit(solution)/shard_map/all_gather | solution.py:72
  9.4 308.3 %all-gather.24.cloned.1.call-start = ((), (), s32[]{:S(2)}) async-start(), calls=%async_computation.29 | async-start | bytes 8650752 | tf_op jit(solution)/shard_map/all_gather | solution.py:76
  140.8 111.1 %all-to-all-start = ((bf16[128,16,128]{2,0,1:T(8,128)(2,1)}), bf16[128,16,128]{2,0,1:T(8,128)(2,1)}, u32[]{:S(2)}, u32[]{:S(2)}) async-start(bf16[128,16,128]{2,0,1:T(8,128)(2,1)} %copy.186), calls=%async_computation | async-start | bytes 1048576 | tf_op jit(solution)/shard_map/all_to_all | solution.py:108
  299.2 261.9 %all-gather.32.cloned.1.call-start = ((), (), s32[]{:S(2)}) async-start(), calls=%async_computation.33 | async-start | bytes 14155776 | tf_op jit(solution)/shard_map/all_gather | solution.py:156
  443.0 265.8 %reduce-scatter.10.cloned.1.call-start = ((), (), s32[]{:S(2)}) async-start(), calls=%async_computation.34 | async-start | bytes 14155776 | tf_op jit(solution)/shard_map/reduce_scatter | solution.py:163
  598.1 278.0 %all-gather.26.cloned.1.call-start = ((), (), s32[]{:S(2)}) async-start(), calls=%async_computation.30 | async-start | bytes 11894784 | tf_op jit(solution)/shard_map/all_gather | solution.py:78
  598.9 369.5 %all-gather.28.cloned.1.call-start = ((), (), s32[]{:S(2)}) async-start(), calls=%async_computation.31 | async-start | bytes 11894784 | tf_op jit(solution)/shard_map/all_gather | solution.py:79
  599.6 461.2 %all-gather.30.cloned.1.call-start = ((), (), s32[]{:S(2)}) async-start(), calls=%async_computation.32 | async-start | bytes 11894784 | tf_op jit(solution)/shard_map/all_gather | solution.py:80
  708.8 174.4 %all-to-all-start.5 = ((bf16[16,72,2048]{2,1,0:T(8,128)(2,1)}), bf16[16,72,2048]{2,1,0:T(8,128)(2,1)}, u32[]{:S(2)}, u32[]{:S(2)}) async-start(bf16[16,72,2048]{2,1,0:T(8,128)(2,1)} %reduce-scatter.10.cloned.1.call-done), calls=%async_computation.6 | async-start | bytes 9437184 | tf_op jit(solution)/shard_map/all_to_all | solution.py:169
  714.5 415.9 %all-gather.36.cloned.1.call-start = ((), (), s32[]{:S(2)}) async-start(), calls=%async_computation.36 | async-start | bytes 2703360 | tf_op jit(solution)/shard_map/all_gather | solution.py:73
  1073.8 120.4 %all-gather.38.cloned.1.call-start = ((), (), s32[]{:S(2)}) async-start(), calls=%async_computation.37 | async-start | bytes 4325376 | tf_op jit(solution)/shard_map/all_gather | solution.py:75
  1074.6 219.3 %all-gather.40.cloned.1.call-start = ((), (), s32[]{:S(2)}) async-start(), calls=%async_computation.38 | async-start | bytes 12976128 | tf_op jit(solution)/shard_map/all_gather | solution.py:72
  1075.1 301.9 %all-gather.42.cloned.1.call-start = ((), (), s32[]{:S(2)}) async-start(), calls=%async_computation.39 | async-start | bytes 8650752 | tf_op jit(solution)/shard_map/all_gather | solution.py:76
  1199.4 111.2 %all-to-all-start.6 = ((bf16[128,16,128]{2,0,1:T(8,128)(2,1)}), bf16[128,16,128]{2,0,1:T(8,128)(2,1)}, u32[]{:S(2)}, u32[]{:S(2)}) async-start(bf16[128,16,128]{2,0,1:T(8,128)(2,1)} %copy.188), calls=%async_computation.7 | async-start | bytes 1048576 | tf_op jit(solution)/shard_map/all_to_all | solution.py:108
  1310.6 19.2 all-to-all-start.8
  1393.4 93.6 %all-to-all-start.11 = ((bf16[16,72,2048]{2,1,0:T(8,128)(2,1)}), bf16[16,72,2048]{2,1,0:T(8,128)(2,1)}, u32[]{:S(2)}, u32[]{:S(2)}) async-start(bf16[16,72,2048]{2,1,0:T(8,128)(2,1)} %bitcast.299), calls=%async_computation.12 | async-start | bytes 9437184 | tf_op jit(solution)/shard_map/all_to_all | solution.py:149
  1400.1 221.3 %all-gather.50.cloned.1.call-start = ((), (), s32[]{:S(2)}) async-start(), calls=%async_computation.43 | async-start | bytes 14155776 | tf_op jit(solution)/shard_map/all_gather | solution.py:156
  1487.0 253.9 %all-gather.48.cloned.1.call-start = ((), (), s32[]{:S(2)}) async-start(), calls=%async_computation.42 | async-start | bytes 14155776 | tf_op jit(solution)/shard_map/all_gather | solution.py:231
  1615.0 219.9 %all-gather.46.cloned.1.call-start = ((), (), s32[]{:S(2)}) async-start(), calls=%async_computation.41 | async-start | bytes 11894784 | tf_op jit(solution)/shard_map/all_gather | solution.py:78
  1615.6 311.6 %all-gather.44.cloned.1.call-start = ((), (), s32[]{:S(2)}) async-start(), calls=%async_computation.40 | async-start | bytes 11894784 | tf_op jit(solution)/shard_map/all_gather | solution.py:79
  1616.1 403.3 %all-gather.34.cloned.1.call-start = ((), (), s32[]{:S(2)}) async-start(), calls=%async_computation.35 | async-start | bytes 11894784 | tf_op jit(solution)/shard_map/all_gather | solution.py:80
  1616.7 514.0 %reduce-scatter.12.cloned.1.call-start = ((), (), s32[]{:S(2)}) async-start(), calls=%async_computation.44 | async-start | bytes 14155776 | tf_op jit(solution)/shard_map/reduce_scatter | solution.py:242
  1780.9 768.2 %reduce-scatter.26.cloned.1.call-start = ((), (), s32[]{:S(2)}) async-start(), calls=%async_computation.51 | async-start | bytes 23789568 | tf_op jit(solution)/shard_map/reduce_scatter | solution.py:335
  1942.8 761.2 %reduce-scatter.24.cloned.1.call-start = ((), (), s32[]{:S(2)}) async-start(), calls=%async_computation.50 | async-start | bytes 23789568 | tf_op jit(solution)/shard_map/reduce_scatter | solution.py:334
  2039.3 916.6 %reduce-scatter.22.cloned.1.call-start = ((), (), s32[]{:S(2)}) async-start(), calls=%async_computation.49 | async-start | bytes 23789568 | tf_op jit(solution)/shard_map/reduce_scatter | solution.py:333
  2130.7 128.0 %all-to-all-start.12 = ((bf16[16,72,2048]{2,1,0:T(8,128)(2,1)}), bf16[16,72,2048]{2,1,0:T(8,128)(2,1)}, u32[]{:S(2)}, u32[]{:S(2)}) async-start(bf16[16,72,2048]{2,1,0:T(8,128)(2,1)} %reduce-scatter.12.cloned.1.call-done), calls=%async_computation.14 | async-start | bytes 9437184 | tf_op jit(solution)/shard_map/all_to_all | solution.py:245
  2335.6 768.5 %reduce-scatter.16.cloned.1.call-start = ((), (), s32[]{:S(2)}) async-start(), calls=%async_computation.46 | async-start | bytes 5406720 | tf_op jit(solution)/shard_map/reduce_scatter | solution.py:328
  2361.4 889.9 %reduce-scatter.18.cloned.1.call-start = ((), (), s32[]{:S(2)}) async-start(), calls=%async_computation.47 | async-start | bytes 8650752 | tf_op jit(solution)/shard_map/reduce_scatter | solution.py:330
  2367.3 1067.6 %reduce-scatter.20.cloned.1.call-start = ((), (), s32[]{:S(2)}) async-start(), calls=%async_computation.48 | async-start | bytes 17301504 | tf_op jit(solution)/shard_map/reduce_scatter | solution.py:331
  2376.5 1311.6 %reduce-scatter.14.cloned.1.call-start = ((), (), s32[]{:S(2)}) async-start(), calls=%async_computation.45 | async-start | bytes 25952256 | tf_op jit(solution)/shard_map/reduce_scatter | solution.py:327
  (85 other events, 9227.5 us)
Sparse Core Ops, SparseCore 0:
  10.9 60.7 all-gather.17
  74.6 60.9 all-gather.19
  138.5 96.8 all-gather.21
  238.1 79.6 all-gather.23
  443.1 117.9 all-gather.31
  598.2 110.5 reduce-scatter.9
  711.6 164.4 all-gather.25
  879.0 89.2 all-gather.27
  971.1 89.5 all-gather.29
  1073.9 56.3 all-gather.35
  1133.2 60.9 all-gather.37
  1197.0 96.8 all-gather.39
  1296.7 80.2 all-gather.41
  1487.1 134.3 all-gather.49
  1622.9 117.9 all-gather.47
  1743.6 91.2 all-gather.45
  1837.6 89.5 all-gather.43
  1929.9 89.5 all-gather.33
  2021.8 108.9 reduce-scatter.11
  2133.5 310.2 reduce-scatter.25
  2446.6 257.3 reduce-scatter.23
  2706.9 248.9 reduce-scatter.21
  2958.8 145.3 reduce-scatter.15
  3106.8 144.4 reduce-scatter.17
  3254.2 180.6 reduce-scatter.19
  3441.7 246.3 reduce-scatter.13
where the time goes:
time: 3710 us; the launch traced here: 3700 us
  waiting for transfers between devices  2630 us (71%)
  blocking collectives  433 us (12%)
  matrix products  320 us (9%)
  local copies, waits for them, and re-layouts  178 us (5%)
  starting transfers between devices  63.1 us (2%)
  other arithmetic  58 us (2%)
    reduce_scatter x1, waiting for transfers between devices, backward(): lax.psum_scatter(query_proj_grad, ('seq', 'fsdp'), scatter_dimension=0, t...  253 us
    reduce_scatter x1, waiting for transfers between devices, backward(): lax.psum_scatter(shared_gate_grad, ('seq', 'fsdp'), scatter_dimension=0,...  252 us
    all_gather x2, waiting for transfers between devices, forward(): lax.all_gather(shared_gate, ('seq', 'fsdp'), axis=0, tiled=True)  215 us
    reduce_scatter x1, waiting for transfers between devices, backward(): lax.psum_scatter(output_proj_grad, ('seq', 'fsdp'), scatter_dimension=0,...  184 us
    dot_general x20, matrix products, contract(): lax.dot_general(left, right, (((left_dim,), (right_dim,)), ((), ())), pre...  181 us
    all_gather x2, waiting for transfers between devices, forward(): lax.all_gather(query_proj, ('seq', 'fsdp'), axis=0, tiled=True)  175 us
    unnamed x3, blocking collectives  171 us
    all_gather x2, waiting for transfers between devices, forward(): lax.all_gather(shared_down, ('seq', 'fsdp'), axis=0, tiled=True)  169 us
  transfers between devices with their start and end apart: 39, of which 33 were waited for; matrix products, arithmetic and copies ran while one was open for 12% of the time, Pallas kernels for 0%

commit v1 on v0

--- a/solution.py
+++ b/solution.py
@@ -1,7 +1,12 @@
+import functools
+
 import jax
 import jax.numpy as jnp
 from jax import lax
+from jax.experimental import pallas as pl
+from jax.experimental.pallas import tpu as pltpu
 from jax.sharding import PartitionSpec as P
+
 
 H = 16
 DN = 128
@@ -337,7 +342,322 @@
     return (input_grad, reduced, expert_gate_grad, expert_up_grad, expert_down_grad)
 
 
-def body(
+def copy_rows(dst, src, rows):
+    def body(i, carry):
+        r = pl.multiple_of(i * 16, 16)
+        dst[pl.ds(r, 16), :] = src[pl.ds(r, 16), :]
+        return carry
+
+    lax.fori_loop(0, rows // 16, body, 0)
+
+
+def gather_all(block, cid):
+    return lax.all_gather(block, ("seq", "fsdp"), axis=0, tiled=False)
+
+
+def scatter_sum(parts, cid):
+    total = lax.psum_scatter(parts, ("seq", "fsdp"), scatter_dimension=0, tiled=False)
+    return total.astype(jnp.float32)
+
+
+def spread_all(blocks, cid):
+    return lax.all_to_all(blocks, ("seq", "fsdp"), split_axis=0, concat_axis=0, tiled=True)
+
+
+def seq_swap(pieces, cid):
+    seq = lax.axis_index("seq")
+    mine = lax.dynamic_index_in_dim(pieces, seq, axis=0, keepdims=False)
+    other = lax.dynamic_index_in_dim(pieces, 1 - seq, axis=0, keepdims=False)
+    return jnp.stack([mine, lax.ppermute(other, "seq", [(0, 1), (1, 0)])])
+
+
+def pass_kernel(x_ref, o_ref):
+    copy_rows(o_ref, x_ref, x_ref.shape[0])
+
+
+def pass_on(block):
+    return pl.pallas_call(
+        pass_kernel, out_shape=jax.ShapeDtypeStruct(block.shape, block.dtype), name="pass_on"
+    )(block)
+
+
+def norm_back(values, gain, upstream):
+    value, pull = jax.vjp(norm_apply, values, gain)
+    return pull(upstream)
+
+
+def block_body(
+    tokens,
+    norm_gain,
+    query_proj,
+    latent_proj,
+    latent_gain,
+    expand_proj,
+    output_proj,
+    mixer_gain,
+    shared_gate,
+    shared_up,
+    shared_down,
+    expert_gate,
+    expert_up,
+    expert_down,
+    doc_starts,
+    routes,
+    gate_levels,
+    cotangent,
+):
+    bf, f32 = jnp.bfloat16, jnp.float32
+    seq = lax.axis_index("seq")
+    fsdp = lax.axis_index("fsdp")
+    both = ("seq", "fsdp")
+    inputs = tokens[0].astype(f32)
+    toks, width = inputs.shape
+    n_dev = 32
+    rows = query_proj.shape[0]
+    latent_rows = expand_proj.shape[0]
+    groups = rows // latent_rows
+    n_q, n_o, n_l = query_proj.shape[1], output_proj.shape[1], latent_proj.shape[1]
+    n_e = expand_proj.shape[1] // groups
+    experts_count = 16
+    capacity = 3 * toks * TOPK // (2 * experts_count)
+
+    chosen = routes[0]
+    levels = gate_levels[0]
+    by_expert = jnp.sum(
+        jnp.where(
+            chosen.T[:, None, :] == jnp.arange(experts_count, dtype=jnp.int32)[None, :, None],
+            levels.T[:, None, :],
+            0,
+        ),
+        axis=0,
+    )
+    info = jnp.concatenate([by_expert, jnp.sum(levels, axis=1)[None]], axis=0).astype(bf)
+    info = jnp.pad(info, ((0, rows - info.shape[0]), (0, 0)))
+    folded = jnp.concatenate(jnp.split(expand_proj, groups, axis=1), axis=0)
+    gains = jnp.stack([norm_gain, mixer_gain, jnp.pad(latent_gain, (0, rows - latent_rows))], axis=1)
+    gains = jnp.pad(gains, ((0, 0), (0, 64 - 3)))
+    packed = jnp.concatenate([query_proj, output_proj, latent_proj, gains, folded, info], axis=1)
+    spots = [0]
+    for part in (n_q, n_o, n_l, 64, n_e, toks):
+        spots.append(spots[-1] + part)
+    weights = gather_all(packed, 1)
+    w_query = weights[:, :, : spots[1]].reshape(width, n_q)
+    w_output = weights[:, :, spots[1] : spots[2]].reshape(width, n_o)
+    w_latent = weights[:, :, spots[2] : spots[3]].reshape(width, n_l)
+    all_gains = weights[:, :, spots[3] : spots[4]].astype(f32)
+    gain_one = all_gains[:, :, 0].reshape(-1)
+    gain_two = all_gains[:, :, 1].reshape(-1)
+    gain_latent = all_gains[:, :latent_rows, 2].reshape(-1)
+    w_expand = weights[:, :, spots[4] : spots[5]].reshape(n_dev, groups, latent_rows, n_e)
+    w_expand = jnp.swapaxes(w_expand, 1, 2).reshape(KVL, groups * n_e)
+    all_info = weights[:, :, spots[5] :].astype(f32)
+
+    n_s = shared_down.shape[0]
+    fill = jnp.zeros((rows, n_dev, 256 - 2 * n_s), bf)
+    gate_up = jnp.concatenate(
+        [shared_gate.reshape(rows, n_dev, n_s), shared_up.reshape(rows, n_dev, n_s), fill], axis=2
+    )
+    w_shared = spread_all(jnp.swapaxes(gate_up, 0, 1), 11).reshape(width, -1)[:, : 2 * n_s]
+
+    cot_all = gather_all(cotangent[0], 3).reshape(-1, width)
+
+    normed = norm_apply(inputs, gain_one).astype(bf)
+    query_raw = jnp.dot(normed, w_query, preferred_element_type=f32).reshape(toks, H, DN + DR)
+    latent_raw = jnp.dot(normed, w_latent, preferred_element_type=f32)
+    latent = latent_raw[:, :KVL]
+    latent_normed = norm_apply(latent, gain_latent).astype(bf)
+    positions = seq * toks + jnp.arange(toks, dtype=jnp.int32)
+    cosine, sine = rotary_tables(positions, DR)
+    query = jnp.concatenate(
+        [query_raw[:, :, :DN], rotate(query_raw[:, :, DN:], cosine[:, None, :], sine[:, None, :])],
+        axis=2,
+    ).astype(bf)
+    key_rotary = rotate(latent_raw[:, KVL:], cosine, sine).astype(bf)
+    own = jnp.concatenate([latent_normed, key_rotary, jnp.zeros((toks, 64), bf)], axis=1)
+    pair = seq_swap(jnp.stack([own, own]), 4)
+    pair = jnp.where(seq == 0, pair, pair[::-1]).reshape(2 * toks, -1)
+    latent_full = pair[:, :KVL]
+    rotary_full = pair[:, KVL : KVL + DR]
+    expanded = jnp.dot(latent_full, w_expand, preferred_element_type=f32).astype(bf)
+    expanded = expanded.reshape(2 * toks, H, DN + DV)
+    keys, values = expanded[:, :, :DN], expanded[:, :, DN:]
+    keys = jnp.concatenate(
+        [keys, jnp.broadcast_to(rotary_full[:, None, :], (2 * toks, H, DR))], axis=2
+    )
+    documents = jnp.cumsum(doc_starts[0])
+    key_spots = jnp.arange(2 * toks)
+    own_documents = lax.dynamic_slice(documents, (seq * toks,), (toks,))
+    allowed = (key_spots[None, :] <= positions[:, None]) & (
+        documents[None, :] == own_documents[:, None]
+    )
+    score_scale = (DN + DR) ** (-0.5)
+    scores = jnp.einsum("qhd,khd->hqk", query, keys, preferred_element_type=f32) * score_scale
+    scores = jnp.where(allowed[None], scores, -1e30)
+    raised = jnp.exp(scores - jnp.max(scores, axis=-1, keepdims=True))
+    soft = raised / jnp.sum(raised, axis=-1, keepdims=True)
+    soft_low = soft.astype(bf)
+    mixed = jnp.einsum("hqk,khd->qhd", soft_low, values, preferred_element_type=f32).astype(bf)
+    attended = mixed.reshape(toks, H * DV)
+    middle = inputs + jnp.dot(attended, w_output, preferred_element_type=f32)
+    normed_two = pass_on(norm_apply(middle, gain_two).astype(bf))
+
+    gathered = gather_all(normed_two, 5)
+    x_all = gathered.reshape(-1, width)
+    level = lax.dynamic_index_in_dim(all_info, fsdp, axis=1, keepdims=False)
+    mask = level > 0
+    share = level / all_info[:, experts_count]
+    slot = jnp.cumsum(mask.astype(jnp.int32), axis=1) - 1
+    pick = mask[:, None, :] & (
+        slot[:, None, :] == jnp.arange(capacity, dtype=jnp.int32)[None, :, None]
+    )
+    share_rows = jnp.sum(jnp.where(pick, share[:, None, :], 0.0), axis=2)
+    pick = pick.astype(bf)
+    expert_rows = jnp.einsum("bst,btd->bsd", pick, gathered, preferred_element_type=f32)
+    expert_rows = expert_rows.astype(bf).reshape(n_dev * capacity, width)
+    gate_weight, up_weight, down_weight = expert_gate[0], expert_up[0], expert_down[0]
+    n_h = gate_weight.shape[1]
+    expert_pre = jnp.dot(expert_rows, gate_weight, preferred_element_type=f32)
+    expert_lift = jnp.dot(expert_rows, up_weight, preferred_element_type=f32)
+    expert_hidden = (sigmoid_linear(expert_pre) * expert_lift).astype(bf)
+    shared_both = jnp.dot(x_all, w_shared, preferred_element_type=f32)
+    shared_pre, shared_lift = shared_both[:, :n_s], shared_both[:, n_s:]
+    shared_hidden = (sigmoid_linear(shared_pre) * shared_lift).astype(bf)
+    spread = jnp.einsum(
+        "bst,bsd->btd",
+        pick,
+        expert_hidden.reshape(n_dev, capacity, n_h),
+        preferred_element_type=f32,
+    )
+    spread = (spread * share[:, :, None]).astype(bf).reshape(-1, n_h)
+    hidden_all = jnp.concatenate([spread, shared_hidden], axis=1)
+    down_all = jnp.concatenate([down_weight, shared_down], axis=0)
+    out_parts = jnp.dot(hidden_all, down_all, preferred_element_type=f32).astype(bf)
+    layer_out = middle + scatter_sum(out_parts.reshape(n_dev, toks, width), 6)
+
+    grad_out = cotangent[0].astype(f32)
+    d_rows = jnp.einsum(
+        "bst,btd->bsd", pick, cot_all.reshape(n_dev, toks, width), preferred_element_type=f32
+    )
+    d_rows = (d_rows * share_rows[:, :, None]).astype(bf).reshape(n_dev * capacity, width)
+    expert_down_grad = contract(expert_hidden, d_rows, 0, 0)
+    d_hidden = contract(d_rows, down_weight, 1, 1)
+    d_pre = (d_hidden * expert_lift * silu_slope(expert_pre)).astype(bf)
+    d_lift = (d_hidden * sigmoid_linear(expert_pre)).astype(bf)
+    expert_gate_grad = contract(expert_rows, d_pre, 0, 0)
+    expert_up_grad = contract(expert_rows, d_lift, 0, 0)
+    d_x = contract(d_pre, gate_weight, 1, 1) + contract(d_lift, up_weight, 1, 1)
+    d_x = d_x.astype(bf).reshape(n_dev, capacity, width)
+    d_x = jnp.einsum("bst,bsd->btd", pick, d_x, preferred_element_type=f32).reshape(-1, width)
+    shared_down_grad = contract(shared_hidden, cot_all, 0, 0)
+    d_shared_hidden = contract(cot_all, shared_down, 1, 1)
+    d_shared_pre = (d_shared_hidden * shared_lift * silu_slope(shared_pre)).astype(bf)
+    d_shared_lift = (d_shared_hidden * sigmoid_linear(shared_pre)).astype(bf)
+    d_shared_both = jnp.concatenate([d_shared_pre, d_shared_lift], axis=1)
+    shared_both_grad = contract(x_all, d_shared_both, 0, 0).astype(bf)
+    d_x = (d_x + contract(d_shared_both, w_shared, 1, 1)).astype(bf)
+    d_normed_two = scatter_sum(d_x.reshape(n_dev, toks, width), 7)
+    shared_both_grad = jnp.pad(shared_both_grad, ((0, 0), (0, 256 - 2 * n_s)))
+    shared_back = spread_all(shared_both_grad.reshape(n_dev, rows, 256), 12)
+    shared_back = jnp.swapaxes(shared_back, 0, 1).astype(f32)
+    shared_gate_grad = shared_back[:, :, :n_s].reshape(rows, n_dev * n_s)
+    shared_up_grad = shared_back[:, :, n_s : 2 * n_s].reshape(rows, n_dev * n_s)
+
+    d_middle_norm, mixer_gain_grad = norm_back(middle, gain_two, d_normed_two)
+    d_middle = grad_out + d_middle_norm
+    d_attn = d_middle.astype(bf)
+    output_proj_grad = contract(attended, d_attn, 0, 0)
+    d_mixed = contract(d_attn, w_output, 1, 1).astype(bf).reshape(toks, H, DV)
+    d_soft = jnp.einsum("qhd,khd->hqk", d_mixed, values, preferred_element_type=f32)
+    delta = jnp.sum(soft * d_soft, axis=-1, keepdims=True)
+    d_scores = (soft * (d_soft - delta)).astype(bf)
+    d_values = jnp.einsum("hqk,qhd->khd", soft_low, d_mixed, preferred_element_type=f32).astype(bf)
+    d_query = (
+        jnp.einsum("hqk,khd->qhd", d_scores, keys, preferred_element_type=f32) * score_scale
+    )
+    d_keys = (
+        jnp.einsum("hqk,qhd->khd", d_scores, query, preferred_element_type=f32) * score_scale
+    )
+    d_query_raw = (
+        jnp.concatenate(
+            [
+                d_query[:, :, :DN],
+                rotate(d_query[:, :, DN:], cosine[:, None, :], -sine[:, None, :]),
+            ],
+            axis=2,
+        )
+        .astype(bf)
+        .reshape(toks, -1)
+    )
+    query_proj_grad = contract(normed, d_query_raw, 0, 0)
+    d_expanded = jnp.concatenate([d_keys[:, :, :DN].astype(bf), d_values], axis=2)
+    d_expanded = d_expanded.reshape(2 * toks, -1)
+    expand_proj_grad = contract(latent_full, d_expanded, 0, 0)
+    d_latent_pair = contract(d_expanded, w_expand, 1, 1)
+    d_rotary_pair = jnp.sum(d_keys[:, :, DN:], axis=1)
+    d_pair = jnp.concatenate(
+        [d_latent_pair, d_rotary_pair, jnp.zeros((2 * toks, 64), f32)], axis=1
+    ).reshape(2, toks, -1)
+    d_pair = jnp.sum(seq_swap(d_pair, 8), axis=0)
+    d_latent_normed = d_pair[:, :KVL]
+    d_key_rotary = rotate(d_pair[:, KVL : KVL + DR], cosine, -sine)
+    d_latent, latent_gain_grad = norm_back(latent, gain_latent, d_latent_normed)
+    d_latent_raw = jnp.concatenate([d_latent, d_key_rotary], axis=1).astype(bf)
+    latent_proj_grad = contract(normed, d_latent_raw, 0, 0)
+    d_normed = contract(d_query_raw, w_query, 1, 1) + contract(d_latent_raw, w_latent, 1, 1)
+    d_inputs, norm_gain_grad = norm_back(inputs, gain_one, d_normed)
+    input_grad = d_middle + d_inputs
+
+    folded_grad = expand_proj_grad.astype(bf).reshape(n_dev, latent_rows, groups, n_e)
+    folded_grad = jnp.swapaxes(folded_grad, 1, 2).reshape(n_dev, rows, n_e)
+    latent_gain_part = jnp.pad(
+        latent_gain_grad.reshape(n_dev, latent_rows), ((0, 0), (0, rows - latent_rows))
+    )
+    gain_parts = jnp.stack(
+        [
+            norm_gain_grad.reshape(n_dev, rows),
+            mixer_gain_grad.reshape(n_dev, rows),
+            latent_gain_part,
+        ],
+        axis=2,
+    )
+    gain_parts = jnp.pad(gain_parts, ((0, 0), (0, 0), (0, 64 - 3))).astype(bf)
+    out_parts_grad = output_proj_grad.astype(bf).reshape(n_dev, rows, n_o)
+    output_grad = scatter_sum(out_parts_grad, 9)
+    grad_parts = jnp.concatenate(
+        [
+            query_proj_grad.astype(bf).reshape(n_dev, rows, n_q),
+            folded_grad,
+            latent_proj_grad.astype(bf).reshape(n_dev, rows, n_l),
+            gain_parts,
+        ],
+        axis=2,
+    )
+    grads = scatter_sum(grad_parts, 10)
+    at_latent = n_q + n_e
+    at_gain = at_latent + n_l
+    expand_out = jnp.concatenate(
+        jnp.split(grads[:, n_q:at_latent], groups, axis=0), axis=1
+    )
+    return (
+        layer_out[None],
+        input_grad[None],
+        grads[:, at_gain],
+        grads[:, :n_q],
+        grads[:, at_latent:at_gain],
+        grads[:latent_rows, at_gain + 2],
+        expand_out,
+        output_grad,
+        grads[:, at_gain + 1],
+        shared_gate_grad,
+        shared_up_grad,
+        shared_down_grad,
+        expert_gate_grad[None],
+        expert_up_grad[None],
+        expert_down_grad[None],
+    )
+
+
+def plain_body(
     tokens,
     norm_gain,
     query_proj,
@@ -374,8 +694,6 @@
     )
     saved = forward(params, tokens, doc_starts, routes, gate_levels)
     layer_out = saved["output"]
-    barrier = lax.optimization_barrier((params, layer_out))
-    saved = forward(barrier[0], tokens, doc_starts, routes, gate_levels)
     input_grad, reduced, expert_gate_grad, expert_up_grad, expert_down_grad = backward(
         saved, cotangent
     )
@@ -436,4 +754,5 @@
         P("fsdp", None, "seq"),
         P("fsdp", "seq", None),
     )
-    return jax.shard_map(body, mesh=mesh, in_specs=in_specs, out_specs=out_specs, check_vma=False)
+    chosen = block_body if dict(mesh.shape) == {"seq": 2, "fsdp": 16} else plain_body
+    return jax.shard_map(chosen, mesh=mesh, in_specs=in_specs, out_specs=out_specs, check_vma=False)

time: 3710 us -> 1330 us (0.36)
  waiting for transfers between devices: 2630 us -> 805 us
  blocking collectives: 433 us -> 0 us
  starting transfers between devices: 63.1 us -> 11.9 us
    reduce_scatter x9 -> x4, waiting for transfers between devices: 1330 us -> 528 us  [scatter_sum(): lax.psum_scatter(parts, ('seq', 'fsdp'), scatter_dimension=0, tiled=False)]
    all_gather x17 -> x3, waiting for transfers between devices: 1080 us -> 276 us  [gather_all(): return lax.all_gather(block, ('seq', 'fsdp'), axis=0, tiled=False)]
    all_to_all x4 -> x0, blocking collectives: 262 us -> none  [the longest x1 125 us: backward(): lax.all_to_all(d_slots.reshape(experts_count, capacity, -1), 'fsdp', spli...]
    all_to_all x13 -> x2, waiting for transfers between devices: 213 us -> 0.01 us  [spread_all(): lax.all_to_all(blocks, ('seq', 'fsdp'), split_axis=0, concat_axis=0, tile...]
    unnamed x3 -> x0, blocking collectives: 171 us -> none
    all_to_all x13 -> x2, starting transfers between devices: 60.7 us -> 8.76 us  [spread_all(): lax.all_to_all(blocks, ('seq', 'fsdp'), split_axis=0, concat_axis=0, tile...]
    gather x5 -> x0, local copies, waits for them, and re-layouts: 45 us -> none  [the longest x1 12.9 us: backward(): jnp.take(d_picked, saved['sources'], axis=0)]
    slice x7 -> x20, local copies, waits for them, and re-layouts: 2.32 us -> 43.8 us  [the longest x1 10.9 us: block_body(): w_query = weights[:, :, :spots[1]].reshape(width, n_q)]
  transfers between devices with their start and end apart: 39 -> 11, of which waited for: 33 -> 5; matrix products, arithmetic and copies ran while one was open for 12% -> 32% of each run, Pallas kernels for 0% -> 0%
where the time goes in v1:
time: 1330 us
  waiting for transfers between devices  805 us (61%)
  matrix products  296 us (22%)
  local copies, waits for them, and re-layouts  164 us (12%)
  other arithmetic  31 us (2%)
  between operations  15.8 us (1%)
    reduce_scatter x4, waiting for transfers between devices, scatter_sum(): lax.psum_scatter(parts, ('seq', 'fsdp'), scatter_dimension=0, tiled=False)  528 us
    all_gather x3, waiting for transfers between devices, gather_all(): return lax.all_gather(block, ('seq', 'fsdp'), axis=0, tiled=False)  276 us
    dot_general x18, matrix products, contract(): lax.dot_general(left, right, (((left_dim,), (right_dim,)), ((), ())), pre...  158 us
    concatenate x1, local copies, waits for them, and re-layouts, block_body(): jnp.concatenate([query_proj_grad.astype(bf).reshape(n_dev, rows, n_q), fo...  28.6 us
  transfers between devices with their start and end apart: 11, of which 5 were waited for; matrix products, arithmetic and copies ran while one was open for 32% of the time, Pallas kernels for 0%

profile of v1, /device:TPU:0, one launch (start us, length us, event | category | flops | bytes accessed | tf_op | source)
XLA Modules:
  0.0 1325.6 jit_solution(3573039112005921541)
XLA Ops:
  17.3 169.3 %all-gather.8.cloned.1.call-done = bf16[2048,6912]{1,0:T(8,128)(2,1)} async-done(((bf16[64,6912]{1,0:T(8,128)(2,1)}), bf16[2048,6912]{1,0:T(8,128)(2,1)}) %all-gather.8.cloned.1.call-update) | async-done | bytes 28311568 | tf_op jit(solution)/shard_map/all_gather | solution.py:355
  194.9 8.7 slice.197
  203.6 10.9 slice.191
  235.3 16.7 %copy.114 = bf16[3072,2048]{1,0:T(8,128)(2,1)} copy(bf16[3072,2048]{0,1:T(8,128)(2,1)} %bitcast.213) | data formatting | bytes 25165824 | tf_op jit(solution)/shard_map/dot_general | solution.py:465
  252.1 8.8 fusion.65
  314.4 12.5 multiply_convert_fusion
  327.0 107.0 %all-gather.10.cloned.1.call-done = bf16[4096,2048]{1,0:T(8,128)(2,1)} async-done(((bf16[128,2048]{1,0:T(8,128)(2,1)}), bf16[4096,2048]{1,0:T(8,128)(2,1)}) %all-gather.10.cloned.1.call-update) | async-done | bytes 16777232 | tf_op jit(solution)/shard_map/all_gather | solution.py:355
  434.0 11.9 convolution_convert_fusion.4
  445.9 13.8 %fusion.11 = f32[2304,704]{0,1:T(8,128)} fusion(bf16[2304,2048]{1,0:T(8,128)(2,1)} %bitcast.229, bf16[1,2048,704]{1,2,0:T(8,128)(2,1)} %param.30), kind=kOutput, calls=%fused_computation.31 | convolution fusion | flops 6643777536 | bytes 18808832 | tf_op jit(solution)/shard_map/dot_general | solution.py:520
  459.7 9.0 fusion.15
  468.7 14.5 %multiply_convert_fusion.2 = (bf16[2304,704]{0,1:T(8,128)(2,1)}, bf16[2304,704]{0,1:T(8,128)(2,1)}, bf16[2304,704]{0,1:T(8,128)(2,1)}) fusion(f32[2304,704]{0,1:T(8,128)} %fusion.15, f32[2304,704]{0,1:T(8,128)} %fusion.11, bf16[2304,2048]{1,0:T(8,128)(2,1)S(1)} %bitcast.228, bf16[1,704,2048]{2,1,0:T(8,128)(2,1)} %param.31), kind=kOutput, calls=%fused_computation.12 | convolution fusion | flops 6668107776 | bytes 35028992 | tf_op jit(solution)/shard_map/dot_general | solution.py:49
  483.2 13.6 %fusion.13 = f32[2304,2048]{1,0:T(8,128)} fusion(bf16[2304,704]{0,1:T(8,128)(2,1)} %get-tuple-element.28, bf16[1,2048,704]{1,2,0:T(8,128)(2,1)S(1)} %copy-done), kind=kOutput, calls=%fused_computation.33 | convolution fusion | flops 6643777536 | bytes 25001984 | tf_op jit(solution)/shard_map/dot_general | solution.py:49
  496.8 14.4 %add_convert_fusion = bf16[2304,2048]{1,0:T(8,128)(2,1)} fusion(f32[2304,2048]{1,0:T(8,128)} %fusion.13, bf16[2304,704]{0,1:T(8,128)(2,1)S(1)} %copy-done.71, bf16[1,2048,704]{1,2,0:T(8,128)(2,1)S(1)} %copy-done.68), kind=kOutput, calls=%fused_computation.3 | convolution fusion | flops 6653214720 | bytes 34439168 | tf_op jit(solution)/shard_map/dot_general | solution.py:49
  511.1 19.3 %fusion.30 = f32[32,128,2048]{2,1,0:T(8,128)} fusion(bf16[32,72,2048]{2,1,0:T(8,128)(2,1)} %bitcast.237, s32[32,128]{1,0:T(8,128)S(1)} %broadcast_add_fusion, pred[32,128]{1,0:T(8,128)(4,1)S(1)} %get-tuple-element.26), kind=kOutput, calls=%fused_computation.78 | convolution fusion | flops 1208549376 | bytes 43012096 | tf_op jit(solution)/shard_map/bst,bsd->btd/dot_general | solution.py:550
  530.4 9.8 fusion.51
  540.2 12.0 multiply_convert_fusion.7
  552.2 19.9 %fusion.1 = bf16[4096,2048]{1,0:T(8,128)(2,1)} fusion(f32[32,128,2048]{2,1,0:T(8,128)} %fusion.30, bf16[4096,88]{0,1:T(8,128)(2,1)S(1)} %get-tuple-element.31, bf16[4096,88]{0,1:T(8,128)(2,1)S(1)} %get-tuple-element.30, bf16[2048,256]{1,0:T(8,128)(2,1)} %bitcast.32), kind=kOutput, calls=%fused_computation.2 | convolution fusion | flops 2972450816 | bytes 52822016 | tf_op jit(solution)/shard_map/dot_general | solution.py:49
  572.2 5.7 copy.117
  586.3 24.5 %convolution_convert_fusion = bf16[4096,2048]{1,0:T(8,128)(2,1)} fusion(bf16[4096,88]{0,1:T(8,128)(2,1)S(1)} %copy-done.23, bf16[4096,704]{0,1:T(8,128)(2,1)} %bitcast.249, bf16[88,2048]{1,0:T(8,128)(2,1)S(1)} %copy-done.69, bf16[704,2048]{1,0:T(8,128)(2,1)} %bitcast.269), kind=kOutput, calls=%fused_computation.5 | convolution fusion | flops 13315407872 | bytes 26509312 | tf_op jit(solution)/shard_map/dot_general | solution.py:534
  610.9 142.8 %reduce-scatter.7.cloned.1.call-done = bf16[1,128,2048]{2,1,0:T(8,128)(2,1)} async-done(((bf16[32,128,2048]{2,1,0:T(8,128)(2,1)}), bf16[1,128,2048]{2,1,0:T(8,128)(2,1)}) %reduce-scatter.7.cloned.1.call-update) | async-done | bytes 524304 | tf_op jit(solution)/shard_map/reduce_scatter | solution.py:359
  755.0 186.0 %reduce-scatter.5.cloned.1.call-done = bf16[1,128,2048]{2,1,0:T(8,128)(2,1)} async-done(((bf16[32,128,2048]{2,1,0:T(8,128)(2,1)}), bf16[1,128,2048]{2,1,0:T(8,128)(2,1)}) %reduce-scatter.5.cloned.1.call-update) | async-done | bytes 524304 | tf_op jit(solution)/shard_map/reduce_scatter | solution.py:359
  949.6 6.3 convolution_convert_fusion.8
  977.5 8.0 reshape.472
  985.5 6.0 copy.126
  994.5 9.1 fusion.127
  1012.5 7.8 convolution_convert_fusion.1
  1020.3 28.6 %concatenate.69 = bf16[32,64,4736]{2,1,0:T(8,128)(2,1)} concatenate(bf16[32,64,3072]{2,1,0:T(8,128)(2,1)} %bitcast.216, bf16[32,64,1024]{2,1,0:T(8,128)(2,1)} %bitcast.238, bf16[32,64,576]{2,1,0:T(8,128)(2,1)S(1)} %bitcast.244, bf16[32,64,64]{2,1,0:T(8,128)(2,1)} %pad.30.clone), dimensions={2} | concatenate | bytes 38797312 | tf_op jit(solution)/shard_map/concatenate | solution.py:626
  1050.2 9.0 convolution_convert_fusion.7
  1066.4 12.1 convolution_bitcast_fusion.2
  1078.5 11.3 convolution_bitcast_fusion
  1093.7 8.9 convolution_bitcast_fusion.1
  1114.5 198.8 %reduce-scatter.9.cloned.1.call-done = bf16[1,64,4736]{2,1,0:T(8,128)(2,1)} async-done(((bf16[32,64,4736]{2,1,0:T(8,128)(2,1)}), bf16[1,64,4736]{2,1,0:T(8,128)(2,1)}) %reduce-scatter.9.cloned.1.call-update) | async-done | bytes 606224 | tf_op jit(solution)/shard_map/reduce_scatter | solution.py:359
  (328 shorter events, 172.9 us)
Async XLA Ops:
  7.2 452.5 %copy-start = (bf16[1,2048,704]{1,2,0:T(8,128)(2,1)S(1)}, bf16[1,2048,704]{1,2,0:T(8,128)(2,1)}, u32[]{:S(2)}) copy-start(bf16[1,2048,704]{1,2,0:T(8,128)(2,1)} %param.29) | copy-start | bytes 8650756
  7.2 179.3 %all-gather.8.cloned.1.call-start = ((), (), s32[]{:S(2)}) async-start(), calls=%async_computation.11 | async-start | bytes 29196288 | tf_op jit(solution)/shard_map/all_gather | solution.py:355
  14.0 300.4 %all-gather.6.cloned.1.call-start = ((), (), s32[]{:S(2)}) async-start(), calls=%async_computation.7 | async-start | bytes 17301504 | tf_op jit(solution)/shard_map/all_gather | solution.py:355
  14.8 419.2 %all-gather.10.cloned.1.call-start = ((), (), s32[]{:S(2)}) async-start(), calls=%async_computation.12 | async-start | bytes 17301504 | tf_op jit(solution)/shard_map/all_gather | solution.py:355
  16.3 207.2 %copy-start.58 = (f32[128]{0:T(128)}, f32[128]{0:T(128)S(1)}, u32[]{:S(2)}) copy-start(f32[128]{0:T(128)S(1)} %fusion.118) | copy-start | bytes 1540
  16.3 207.2 %copy-start.60 = (f32[32]{0:T(128)}, f32[32]{0:T(128)S(1)}, u32[]{:S(2)}) copy-start(f32[32]{0:T(128)S(1)} %multiply_power_fusion) | copy-start | bytes 388
  16.5 178.4 %copy-start.64 = (f32[128]{0:T(128)}, f32[128]{0:T(128)S(1)}, u32[]{:S(2)}) copy-start(f32[128]{0:T(128)S(1)} %fusion.38) | copy-start | bytes 1540
  16.5 235.5 %copy-start.50 = (f32[128]{0:T(128)}, f32[128]{0:T(128)S(1)}, u32[]{:S(2)}) copy-start(f32[128]{0:T(128)S(1)} %fusion.101) | copy-start | bytes 1540
  220.3 31.8 %copy-start.32 = (f32[2048]{0:T(1024)}, f32[2048]{0:T(1024)S(1)}, u32[]{:S(2)}) copy-start(f32[2048]{0:T(1024)S(1)} %mul.395) | copy-start | bytes 24580
  224.2 37.6 %copy-start.43 = (f32[128,32]{0,1:T(8,128)}, f32[128,32]{0,1:T(8,128)S(1)}, u32[]{:S(2)}) copy-start(f32[128,32]{0,1:T(8,128)S(1)} %get-tuple-element.58) | copy-start | bytes 49156
  225.4 37.1 %collective-permute-start = (bf16[128,640]{0,1:T(8,128)(2,1)}, bf16[128,640]{0,1:T(8,128)(2,1)}, u32[]{:S(2)}, u32[]{:S(2)}) collective-permute-start(bf16[128,640]{0,1:T(8,128)(2,1)} %get-tuple-element.52), channel_id=1, source_target_pairs={{0,16},{16,0},{1,17},{17,1},{2,18},{18,2},{3,19},{19,3},{4,20},{20... | collective-permute-start | bytes 491528 | tf_op jit(solution)/shard_map/ppermute | solution.py:371
  306.0 224.4 %all-to-all-start = ((bf16[32,64,256]{2,1,0:T(8,128)(2,1)}), bf16[32,64,256]{2,1,0:T(8,128)(2,1)}, u32[]{:S(2)}, u32[]{:S(2)}) async-start(bf16[32,64,256]{2,1,0:T(8,128)(2,1)} %copy.119), calls=%async_computation | async-start | bytes 2097152 | tf_op jit(solution)/shard_map/all_to_all | solution.py:364
  309.4 444.3 %reduce-scatter.7.cloned.1.call-start = ((), (), s32[]{:S(2)}) async-start(), calls=%async_computation.8 | async-start | bytes 17301504 | tf_op jit(solution)/shard_map/reduce_scatter | solution.py:359
  445.9 22.8 %slice-start.4 = ((s8[9437184]{0:T(1024)(128)(4,1)}), s8[4194304]{0:T(1024)(128)(4,1)S(1)}, s32[]{:S(2)}) async-start(s8[9437184]{0:T(1024)(128)(4,1)} %bitcast.226), calls=%async_computation.17 | async-start | bytes 8388608
  445.9 22.8 %slice-start.5 = ((s8[9437184]{0:T(1024)(128)(4,1)}), s8[4194304]{0:T(1024)(128)(4,1)S(1)}, s32[]{:S(2)}) async-start(s8[9437184]{0:T(1024)(128)(4,1)} %bitcast.226), calls=%async_computation.18 | async-start | bytes 8388608
  552.2 19.9 %copy-start.29 = (bf16[4096,88]{0,1:T(8,128)(2,1)}, bf16[4096,88]{0,1:T(8,128)(2,1)S(1)}, u32[]{:S(2)}) copy-start(bf16[4096,88]{0,1:T(8,128)(2,1)S(1)} %get-tuple-element.31) | copy-start | bytes 2162692
  572.1 369.0 %reduce-scatter.5.cloned.1.call-start = ((), (), s32[]{:S(2)}) async-start(), calls=%async_computation.6 | async-start | bytes 17301504 | tf_op jit(solution)/shard_map/reduce_scatter | solution.py:359
  610.8 142.9 %copy-start.9 = (f32[128,2048]{1,0:T(8,128)S(1)}, f32[128,2048]{1,0:T(8,128)}, u32[]{:S(2)}) copy-start(f32[128,2048]{1,0:T(8,128)} %copy-done.8) | copy-start | bytes 3145732
  610.8 142.9 %copy-start.46 = (f32[2048]{0:T(1024)S(1)}, f32[2048]{0:T(1024)}, u32[]{:S(2)}) copy-start(f32[2048]{0:T(1024)} %mul.423) | copy-start | bytes 24580
  610.8 142.9 %copy-start.57 = (f32[128]{0:T(128)S(1)}, f32[128]{0:T(128)}, u32[]{:S(2)}) copy-start(f32[128]{0:T(128)} %copy-done.56) | copy-start | bytes 1540
  610.8 144.3 %copy-start.63 = (f32[128]{0:T(128)S(1)}, f32[128]{0:T(128)}, u32[]{:S(2)}) copy-start(f32[128]{0:T(128)} %copy-done.62) | copy-start | bytes 1540
  610.8 330.3 %copy-start.22 = (bf16[1,128,2048]{2,1,0:T(8,128)(2,1)S(1)}, bf16[1,128,2048]{2,1,0:T(8,128)(2,1)}, u32[]{:S(2)}) copy-start(bf16[1,128,2048]{2,1,0:T(8,128)(2,1)} %param.35) | copy-start | bytes 1572868
  610.8 332.8 %copy-start.15 = (bf16[16,128,128]{2,1,0:T(8,128)(2,1)S(1)}, bf16[16,128,128]{2,1,0:T(8,128)(2,1)}, u32[]{:S(2)}) copy-start(bf16[16,128,128]{2,1,0:T(8,128)(2,1)} %copy-done.14) | copy-start | bytes 1572868
  610.8 501.9 %reduce-scatter.11.cloned.1.call-start = ((), (), s32[]{:S(2)}) async-start(), calls=%async_computation.10 | async-start | bytes 8650752 | tf_op jit(solution)/shard_map/reduce_scatter | solution.py:359
  949.3 364.0 %reduce-scatter.9.cloned.1.call-start = ((), (), s32[]{:S(2)}) async-start(), calls=%async_computation.9 | async-start | bytes 20004864 | tf_op jit(solution)/shard_map/reduce_scatter | solution.py:359
  972.3 19.3 %collective-permute-start.1 = (f32[128,640]{0,1:T(8,128)S(1)}, f32[128,640]{0,1:T(8,128)}, u32[]{:S(2)}, u32[]{:S(2)}) collective-permute-start(f32[128,640]{0,1:T(8,128)S(1)} %bitcast.263), channel_id=1, source_target_pairs={{0,16},{16,0},{1,17},{17,1},{2,18},{18,2},{3,19},{19,3},{4,20},{20... | collective-permute-start | bytes 983048 | tf_op jit(solution)/shard_map/ppermute | solution.py:371
  1060.9 41.6 %all-to-all-start.1 = ((bf16[32,64,256]{2,1,0:T(8,128)(2,1)}), bf16[32,64,256]{2,1,0:T(8,128)(2,1)}, u32[]{:S(2)}, u32[]{:S(2)}) async-start(bf16[32,64,256]{2,1,0:T(8,128)(2,1)} %bitcast.64), calls=%async_computation.5 | async-start | bytes 2097152 | tf_op jit(solution)/shard_map/all_to_all | solution.py:364
  1066.3 23.5 %slice-start = ((s8[16777216]{0:T(1024)(128)(4,1)}), s8[4194304]{0:T(1024)(128)(4,1)S(1)}, s32[]{:S(2)}) async-start(s8[16777216]{0:T(1024)(128)(4,1)} %bitcast.207), calls=%async_computation.13 | async-start | bytes 8388608
  1066.3 23.5 %slice-start.1 = ((s8[16777216]{0:T(1024)(128)(4,1)}), s8[4194304]{0:T(1024)(128)(4,1)S(1)}, s32[]{:S(2)}) async-start(s8[16777216]{0:T(1024)(128)(4,1)} %bitcast.207), calls=%async_computation.14 | async-start | bytes 8388608
  1066.3 27.3 %slice-start.7 = ((s8[9437184]{0:T(1024)(128)(4,1)}), s8[4194304]{0:T(1024)(128)(4,1)S(1)}, s32[]{:S(2)}) async-start(s8[9437184]{0:T(1024)(128)(4,1)} %bitcast.232), calls=%async_computation.20 | async-start | bytes 8388608
  1066.4 27.3 %slice-start.8 = ((s8[9437184]{0:T(1024)(128)(4,1)}), s8[4194304]{0:T(1024)(128)(4,1)S(1)}, s32[]{:S(2)}) async-start(s8[9437184]{0:T(1024)(128)(4,1)} %bitcast.232), calls=%async_computation.21 | async-start | bytes 8388608
  1109.6 208.7 %copy-start.1 = (bf16[1,2048,704]{1,2,0:T(8,128)(2,1)S(1)}, bf16[1,2048,704]{1,2,0:T(8,128)(2,1)}, u32[]{:S(2)}) copy-start(bf16[1,2048,704]{1,2,0:T(8,128)(2,1)} %param.29) | copy-start | bytes 8650756
  (62 other events, 374.4 us)
Sparse Core Ops, SparseCore 0:
  14.1 172.3 all-gather.7
  189.4 116.5 all-gather.5
  309.5 124.4 all-gather.9
  572.3 181.3 reduce-scatter.6
  755.8 185.2 reduce-scatter.4
  949.4 154.9 reduce-scatter.10
  1106.7 206.6 reduce-scatter.8

commit v2 on v1

--- a/solution.py
+++ b/solution.py
@@ -342,43 +342,653 @@
     return (input_grad, reduced, expert_gate_grad, expert_up_grad, expert_down_grad)
 
 
-def copy_rows(dst, src, rows):
-    def body(i, carry):
-        r = pl.multiple_of(i * 16, 16)
-        dst[pl.ds(r, 16), :] = src[pl.ds(r, 16), :]
+MESH = pl.DeviceIdType.MESH
+
+def busy(micros):
+    return pl.CostEstimate(flops=0, bytes_accessed=int(micros * 3.5e6), transcendentals=0)
+
+
+def coords():
+    seq = lax.axis_index("seq")
+    fsdp = lax.axis_index("fsdp")
+    return seq, lax.rem(fsdp // 2, 2), fsdp // 4, lax.rem(fsdp, 2)
+
+def device(x, y, z, c):
+    return (x, (z * 2 + y) * 2 + c)
+
+def place(x, y, z, c):
+    return x * 16 + z * 4 + y * 2 + c
+
+def greet(x, y, z, c):
+    bar = pltpu.get_barrier_semaphore()
+    for dev in (device(1 - x, y, z, c), device(x, 1 - y, z, c), device(x, y, z, 1 - c)):
+        pl.semaphore_signal(bar, inc=1, device_id=dev, device_id_type=MESH)
+    @pl.when(z > 0)
+    def _():
+        pl.semaphore_signal(bar, inc=1, device_id=device(x, y, z - 1, c), device_id_type=MESH)
+    @pl.when(z < 3)
+    def _():
+        pl.semaphore_signal(bar, inc=1, device_id=device(x, y, z + 1, c), device_id_type=MESH)
+    pl.semaphore_wait(bar, jnp.where((z > 0) & (z < 3), 5, 4))
+
+def remote(src, dst, ss, rs, dev):
+    return pltpu.make_async_remote_copy(src_ref=src, dst_ref=dst, send_sem=ss, recv_sem=rs, device_id=dev, device_id_type=MESH)
+
+def near_order(z):
+    w = jnp.where
+    first = w(z == 0, 1, w(z == 1, 0, w(z == 2, 1, 2)))
+    second = w(z == 0, 2, w(z == 1, 2, w(z == 2, 3, 1)))
+    third = w(z == 0, 3, w(z == 1, 3, 0))
+    return (first, second, third)
+
+def ag_kernel(half, x_ref, o_ref, zs, zr, xs, xr, ys, yr, das, dar, dbs, dbr, cs, cr, ls):
+    x, y, z, c = coords()
+    greet(x, y, z, c)
+    xm, ym, cm = device(1 - x, y, z, c), device(x, 1 - y, z, c), device(x, y, z, 1 - c)
+    lo, hi = pl.ds(0, half), pl.ds(half, half)
+    me = o_ref.at[place(x, y, z, c)]
+    order = (z,) + near_order(z)
+    sends = []
+    local = pltpu.make_async_copy(x_ref, me, ls)
+    local.start()
+    def up(src, zz, sem):
+        return remote(src, o_ref.at[place(x, y, zz, c)], zs.at[sem], zr.at[zz], device(x, y, z + 1, c))
+    def down(src, zz, sem):
+        return remote(src, o_ref.at[place(x, y, zz, c)], zs.at[sem], zr.at[zz], device(x, y, z - 1, c))
+    @pl.when(z < 3)
+    def _():
+        up(x_ref, z, 0).start()
+    @pl.when(z > 0)
+    def _():
+        down(x_ref, z, 1).start()
+    def blk(dx, dy, zz, cc=None):
+        return o_ref.at[place(jnp.abs(x - dx), jnp.abs(y - dy), zz, c if cc is None else cc)]
+    def xsend(j):
+        b = x_ref if j == 0 else blk(0, 0, order[j])
+        return remote(b, blk(0, 0, order[j]), xs.at[j], xr.at[j], xm)
+    def ysend(j):
+        b = x_ref if j == 0 else blk(0, 0, order[j])
+        return remote(b, blk(0, 0, order[j]), ys.at[j], yr.at[j], ym)
+    def xrecv(j):
+        b = blk(1, 0, order[j])
+        return remote(b, b, xs.at[j], xr.at[j], xm)
+    def yrecv(j):
+        b = blk(0, 1, order[j])
+        return remote(b, b, ys.at[j], yr.at[j], ym)
+    def dasend(j):
+        b = blk(1, 0, order[j]).at[lo]
+        return remote(b, b, das.at[j], dar.at[j], ym)
+    def dbsend(j):
+        b = blk(0, 1, order[j]).at[hi]
+        return remote(b, b, dbs.at[j], dbr.at[j], xm)
+    def darecv(j):
+        b = blk(1, 1, order[j]).at[lo]
+        return remote(b, b, das.at[j], dar.at[j], ym)
+    def dbrecv(j):
+        b = blk(1, 1, order[j]).at[hi]
+        return remote(b, b, dbs.at[j], dbr.at[j], xm)
+    def csend(j, q):
+        dx, dy = q % 2, q // 2
+        b = blk(dx, dy, order[j])
+        src = x_ref if (j == 0 and q == 0) else b
+        return remote(src, b, cs.at[j * 4 + q], cr.at[j * 4 + q], cm)
+    def crecv(j, q):
+        b = blk(q % 2, q // 2, order[j], 1 - c)
+        return remote(b, b, cs.at[j * 4 + q], cr.at[j * 4 + q], cm)
+    def second(j):
+        xrecv(j).wait_recv()
+        dasend(j).start()
+        csend(j, 1).start()
+        yrecv(j).wait_recv()
+        dbsend(j).start()
+        csend(j, 2).start()
+    def third(j):
+        darecv(j).wait_recv()
+        dbrecv(j).wait_recv()
+        csend(j, 3).start()
+    xsend(0).start()
+    ysend(0).start()
+    csend(0, 0).start()
+    for j in (1, 2, 3):
+        zz = order[j]
+        b = o_ref.at[place(x, y, zz, c)]
+        remote(b, b, zs.at[0], zr.at[zz], cm).wait_recv()
+        @pl.when((zz < z) & (z < 3))
+        def _():
+            up(b, zz, j + 1).start()
+        @pl.when((zz > z) & (z > 0))
+        def _():
+            down(b, zz, j + 1).start()
+        xsend(j).start()
+        ysend(j).start()
+        csend(j, 0).start()
+        second(j - 1)
+        if j > 1:
+            third(j - 2)
+    second(3)
+    third(2)
+    third(3)
+    local.wait()
+    @pl.when(z < 3)
+    def _():
+        up(x_ref, z, 0).wait_send()
+    @pl.when(z > 0)
+    def _():
+        down(x_ref, z, 1).wait_send()
+    for j in range(4):
+        if j:
+            zz = order[j]
+            b = o_ref.at[place(x, y, zz, c)]
+            @pl.when((zz < z) & (z < 3))
+            def _():
+                up(b, zz, j + 1).wait_send()
+            @pl.when((zz > z) & (z > 0))
+            def _():
+                down(b, zz, j + 1).wait_send()
+        xsend(j).wait_send()
+        ysend(j).wait_send()
+        dasend(j).wait_send()
+        dbsend(j).wait_send()
+        for q in range(4):
+            csend(j, q).wait_send()
+            crecv(j, q).wait_recv()
+
+DMA = pltpu.SemaphoreType.DMA
+
+def gather_all(block, cid):
+    rows, cols = block.shape
+    grouped = (rows // 8, 8, cols)
+    out = pl.pallas_call(
+        functools.partial(ag_kernel, rows // 16),
+        out_shape=jax.ShapeDtypeStruct((32,) + grouped, block.dtype),
+        in_specs=[pl.BlockSpec(memory_space=pl.ANY)],
+        out_specs=pl.BlockSpec(memory_space=pl.ANY),
+        scratch_shapes=[DMA((5,)), DMA((4,))] + [DMA((4,))] * 8 + [DMA((16,)), DMA((16,)), DMA],
+        compiler_params=pltpu.CompilerParams(
+            collective_id=cid, has_side_effects=True, vmem_limit_bytes=60 * 2**20
+        ),
+        cost_estimate=busy(20 + block.size * block.dtype.itemsize / 8e3 ),
+        name="gather_rows",
+    )(block.reshape(grouped))
+    return out
+
+
+def far_order(z):
+    w = jnp.where
+    first = w(z < 2, 3, 0)
+    second = w(z == 0, 2, w(z == 1, 0, w(z == 2, 3, 1)))
+    third = w(z == 0, 1, w(z == 1, 2, w(z == 2, 1, 2)))
+    return (first, second, third, z)
+
+def rs_kernel(half, p_ref, o_ref, acc, cl, lxa, lya2, lyb, lxb2, zl, ls, cs, cr, xas, xar, ya2s, ya2r, ybs, ybr, xb2s, xb2r, zs, zr):
+    x, y, z, c = coords()
+    greet(x, y, z, c)
+    xm, ym, cm = device(1 - x, y, z, c), device(x, 1 - y, z, c), device(x, y, z, 1 - c)
+    order = far_order(z)
+    rows = 2 * half
+    lo, hi = pl.ds(0, half), pl.ds(half, half)
+    def add(dst, at, src, src_at, count):
+        def body(i, carry):
+            d = dst.at[pl.ds(at + 2 * i, 2)]
+            s = src.at[pl.ds(src_at + 2 * i, 2)]
+            d[...] = (d[...].astype(jnp.float32) + s[...].astype(jnp.float32)).astype(d.dtype)
+            return carry
+        lax.fori_loop(0, count // 2, body, 0)
+    def blk(q, zz, cc):
+        return p_ref.at[place(jnp.abs(x - q % 2), jnp.abs(y - q // 2), zz, cc)]
+    def load(j, q):
+        return pltpu.make_async_copy(blk(q, order[j], c), acc.at[j, q], ls.at[j * 4 + q])
+    def csend(j, q):
+        return remote(blk(q, order[j], 1 - c), cl.at[j, q], cs.at[j * 4 + q], cr.at[j * 4 + q], cm)
+    def xa(j, i):
+        return remote(acc.at[j, 1 + 2 * i, lo], lxa.at[j, i], xas.at[j, i], xar.at[j, i], xm)
+    def yb(j, i):
+        return remote(acc.at[j, 2 + i, hi], lyb.at[j, i], ybs.at[j, i], ybr.at[j, i], ym)
+    def ya2(j):
+        return remote(acc.at[j, 2, lo], lya2.at[j], ya2s.at[j], ya2r.at[j], ym)
+    def xb2(j):
+        return remote(acc.at[j, 1, hi], lxb2.at[j], xb2s.at[j], xb2r.at[j], xm)
+    firsts = (1, 3, 2, 0)
+    for j in range(4):
+        for q in firsts:
+            csend(j, q).start()
+            load(j, q).start()
+    def one(j):
+        for q in firsts:
+            load(j, q).wait()
+            csend(j, q).wait_recv()
+            add(acc.at[j, q], 0, cl.at[j, q], 0, rows)
+            if q == 1:
+                xa(j, 0).start()
+            if q == 3:
+                xa(j, 1).start()
+                yb(j, 1).start()
+            if q == 2:
+                yb(j, 0).start()
+    def two(j):
+        xa(j, 1).wait_recv()
+        add(acc.at[j, 2], 0, lxa.at[j, 1], 0, half)
+        ya2(j).start()
+        yb(j, 1).wait_recv()
+        add(acc.at[j, 1], half, lyb.at[j, 1], 0, half)
+        xb2(j).start()
+        xa(j, 0).wait_recv()
+        add(acc.at[j, 0], 0, lxa.at[j, 0], 0, half)
+        yb(j, 0).wait_recv()
+        add(acc.at[j, 0], half, lyb.at[j, 0], 0, half)
+    def zin(slot):
+        return remote(zl.at[slot], zl.at[slot], zs.at[0], zr.at[slot], cm)
+    def zout_up(j):
+        return remote(acc.at[j, 0], zl.at[order[j]], zs.at[j], zr.at[order[j]], device(x, y, z + 1, c))
+    def zout_down(j):
+        slot = jnp.where(order[j] == z - 1, 4, order[j])
+        return remote(acc.at[j, 0], zl.at[slot], zs.at[j], zr.at[slot], device(x, y, z - 1, c))
+    def three(j):
+        ya2(j).wait_recv()
+        add(acc.at[j, 0], 0, lya2.at[j], 0, half)
+        xb2(j).wait_recv()
+        add(acc.at[j, 0], half, lxb2.at[j], 0, half)
+        zz = order[j]
+        if j < 3:
+            @pl.when(((zz > z) & (z > 0)) | ((zz < z) & (z < 3)))
+            def _():
+                zin(zz).wait_recv()
+                add(acc.at[j, 0], 0, zl.at[zz], 0, rows)
+            @pl.when(zz > z)
+            def _():
+                zout_up(j).start()
+            @pl.when(zz < z)
+            def _():
+                zout_down(j).start()
+        else:
+            @pl.when(z > 0)
+            def _():
+                zin(z).wait_recv()
+                add(acc.at[j, 0], 0, zl.at[z], 0, rows)
+            @pl.when(z < 3)
+            def _():
+                zin(4).wait_recv()
+                add(acc.at[j, 0], 0, zl.at[4], 0, rows)
+            def body(i, carry):
+                o_ref[pl.ds(2 * i, 2)] = acc[3, 0, pl.ds(2 * i, 2)].astype(o_ref.dtype)
+                return carry
+            lax.fori_loop(0, rows // 2, body, 0)
+    one(0)
+    one(1)
+    two(0)
+    one(2)
+    three(0)
+    two(1)
+    one(3)
+    three(1)
+    two(2)
+    three(2)
+    two(3)
+    three(3)
+    for j in range(4):
+        for q in range(4):
+            csend(j, q).wait_send()
+        for i in range(2):
+            xa(j, i).wait_send()
+            yb(j, i).wait_send()
+        ya2(j).wait_send()
+        xb2(j).wait_send()
+        if j < 3:
+            zz = order[j]
+            @pl.when(zz > z)
+            def _():
+                zout_up(j).wait_send()
+            @pl.when(zz < z)
+            def _():
+                zout_down(j).wait_send()
+
+def scatter_sum(parts, cid):
+    _, rows, cols = parts.shape
+    bf = parts.dtype
+    whole, half = (rows // 8, 8, cols), (rows // 16, 8, cols)
+    out = pl.pallas_call(
+        functools.partial(rs_kernel, rows // 16),
+        out_shape=jax.ShapeDtypeStruct(whole, jnp.float32),
+        in_specs=[pl.BlockSpec(memory_space=pl.ANY)],
+        out_specs=pl.BlockSpec(memory_space=pltpu.VMEM),
+        scratch_shapes=[
+            pltpu.VMEM((4, 4) + whole, bf),
+            pltpu.VMEM((4, 4) + whole, bf),
+            pltpu.VMEM((4, 2) + half, bf),
+            pltpu.VMEM((4,) + half, bf),
+            pltpu.VMEM((4, 2) + half, bf),
+            pltpu.VMEM((4,) + half, bf),
+            pltpu.VMEM((5,) + whole, bf),
+            DMA((16,)), DMA((16,)), DMA((16,)), DMA((4, 2)), DMA((4, 2)), DMA((4,)), DMA((4,)),
+            DMA((4, 2)), DMA((4, 2)), DMA((4,)), DMA((4,)), DMA((3,)), DMA((5,)),
+        ],
+        compiler_params=pltpu.CompilerParams(
+            collective_id=cid, has_side_effects=True, vmem_limit_bytes=60 * 2**20
+        ),
+        cost_estimate=busy(20 + rows * cols * bf.itemsize / 8e3),
+        name="scatter_sum",
+    )(parts.reshape((32,) + whole))
+    return out.reshape(rows, cols)
+
+
+def spread_kernel(x_ref, o_ref, ls, ss, rs):
+    x, y, z, c = coords()
+    me = place(x, y, z, c)
+    n_dev = x_ref.shape[0]
+
+    def far(k):
+        kx, kz, ky, kc = k // 16, lax.rem(k // 4, 4), lax.rem(k // 2, 2), lax.rem(k, 2)
+        return jnp.abs(x - kx), jnp.abs(y - ky), lax.rem(z + kz, 4), jnp.abs(c - kc)
+
+    bar = pltpu.get_barrier_semaphore()
+
+    def greet_one(k, carry):
+        pl.semaphore_signal(bar, inc=1, device_id=device(*far(k)), device_id_type=MESH)
         return carry
 
-    lax.fori_loop(0, rows // 16, body, 0)
-
-
-def gather_all(block, cid):
-    return lax.all_gather(block, ("seq", "fsdp"), axis=0, tiled=False)
-
-
-def scatter_sum(parts, cid):
-    total = lax.psum_scatter(parts, ("seq", "fsdp"), scatter_dimension=0, tiled=False)
-    return total.astype(jnp.float32)
+    lax.fori_loop(1, n_dev, greet_one, 0)
+
+    pl.semaphore_wait(bar, n_dev - 1)
+
+    def send(k):
+        to = far(k)
+        return remote(x_ref.at[place(*to)], o_ref.at[me], ss.at[k], rs.at[k], device(*to))
+
+    def start(k, carry):
+        send(k).start()
+        return carry
+
+    lax.fori_loop(1, n_dev, start, 0)
+    local = pltpu.make_async_copy(x_ref.at[me], o_ref.at[me], ls)
+    local.start()
+    local.wait()
+
+    def finish(k, carry):
+        send(k).wait()
+        return carry
+
+    lax.fori_loop(1, n_dev, finish, 0)
 
 
 def spread_all(blocks, cid):
-    return lax.all_to_all(blocks, ("seq", "fsdp"), split_axis=0, concat_axis=0, tiled=True)
+    count, rows, cols = blocks.shape
+    grouped = (count, rows // 8, 8, cols)
+    out = pl.pallas_call(
+        spread_kernel,
+        out_shape=jax.ShapeDtypeStruct(grouped, blocks.dtype),
+        in_specs=[pl.BlockSpec(memory_space=pl.ANY)],
+        out_specs=pl.BlockSpec(memory_space=pl.ANY),
+        scratch_shapes=[DMA, DMA((32,)), DMA((32,))],
+        compiler_params=pltpu.CompilerParams(
+            collective_id=cid, has_side_effects=True, vmem_limit_bytes=60 * 2**20
+        ),
+        cost_estimate=busy(25),
+        name="spread_all",
+    )(blocks.reshape(grouped))
+    return out.reshape(blocks.shape)
+
+
+def swap_kernel(x_ref, o_ref, ls, ss, rs):
+    x, y, z, c = coords()
+    mate = device(1 - x, y, z, c)
+    bar = pltpu.get_barrier_semaphore()
+    pl.semaphore_signal(bar, inc=1, device_id=mate, device_id_type=MESH)
+    pl.semaphore_wait(bar, 1)
+    out = remote(x_ref.at[1 - x], o_ref.at[1], ss, rs, mate)
+    out.start()
+    local = pltpu.make_async_copy(x_ref.at[x], o_ref.at[0], ls)
+    local.start()
+    local.wait()
+    out.wait()
 
 
 def seq_swap(pieces, cid):
-    seq = lax.axis_index("seq")
-    mine = lax.dynamic_index_in_dim(pieces, seq, axis=0, keepdims=False)
-    other = lax.dynamic_index_in_dim(pieces, 1 - seq, axis=0, keepdims=False)
-    return jnp.stack([mine, lax.ppermute(other, "seq", [(0, 1), (1, 0)])])
-
-
-def pass_kernel(x_ref, o_ref):
-    copy_rows(o_ref, x_ref, x_ref.shape[0])
-
-
-def pass_on(block):
+    count, rows, cols = pieces.shape
+    grouped = (count, rows // 8, 8, cols)
+    out = pl.pallas_call(
+        swap_kernel,
+        out_shape=jax.ShapeDtypeStruct(grouped, pieces.dtype),
+        in_specs=[pl.BlockSpec(memory_space=pl.ANY)],
+        out_specs=pl.BlockSpec(memory_space=pl.ANY),
+        scratch_shapes=[DMA, DMA, DMA],
+        compiler_params=pltpu.CompilerParams(
+            collective_id=cid, has_side_effects=True, vmem_limit_bytes=60 * 2**20
+        ),
+        cost_estimate=busy(8),
+        name="seq_swap",
+    )(pieces.reshape(grouped))
+    return out.reshape(pieces.shape)
+
+
+def columns_kernel(x_ref, w_ref, o_ref):
+    o_ref[...] = jnp.dot(x_ref[...], w_ref[...], preferred_element_type=jnp.float32)
+
+
+def times_columns(rows_in, weights, first, count, tile):
+    m, k = rows_in.shape
     return pl.pallas_call(
-        pass_kernel, out_shape=jax.ShapeDtypeStruct(block.shape, block.dtype), name="pass_on"
-    )(block)
+        columns_kernel,
+        grid=(count,),
+        out_shape=jax.ShapeDtypeStruct((m, count * tile), jnp.float32),
+        in_specs=[
+            pl.BlockSpec((m, k), lambda i: (0, 0)),
+            pl.BlockSpec((k, tile), lambda i: (0, first + i)),
+        ],
+        out_specs=pl.BlockSpec((m, tile), lambda i: (0, i)),
+        compiler_params=pltpu.CompilerParams(vmem_limit_bytes=48 * 2**20),
+        name="times_columns",
+    )(rows_in, weights)
+
+
+def rows_kernel(x_ref, w_ref, o_ref):
+    o_ref[...] = contract(x_ref[...], w_ref[...], 1, 1)
+
+
+def times_rows(rows_in, weights, at, width, tile):
+    m = rows_in.shape[0]
+    k = weights.shape[0]
+    return pl.pallas_call(
+        rows_kernel,
+        grid=(k // tile,),
+        out_shape=jax.ShapeDtypeStruct((m, k), jnp.float32),
+        in_specs=[
+            pl.BlockSpec((m, width), lambda i: (0, 0)),
+            pl.BlockSpec((tile, width), lambda i: (i, at)),
+        ],
+        out_specs=pl.BlockSpec((m, tile), lambda i: (0, i)),
+        compiler_params=pltpu.CompilerParams(vmem_limit_bytes=48 * 2**20),
+        name="times_rows",
+    )(rows_in, weights)
+
+
+def expand_kernel(x_ref, w_ref, o_ref):
+    weight = w_ref[...].reshape(x_ref.shape[1], w_ref.shape[2])
+    o_ref[...] = jnp.dot(x_ref[...], weight, preferred_element_type=jnp.float32).astype(o_ref.dtype)
+
+
+def times_folded(rows_in, weights, fold, at, width):
+    m, k = rows_in.shape
+    groups = weights.shape[1] // fold
+    return pl.pallas_call(
+        expand_kernel,
+        grid=(groups,),
+        out_shape=jax.ShapeDtypeStruct((m, groups * width), jnp.bfloat16),
+        in_specs=[
+            pl.BlockSpec((m, k), lambda g: (0, 0)),
+            pl.BlockSpec((weights.shape[0], fold, width), lambda g: (0, g, at)),
+        ],
+        out_specs=pl.BlockSpec((m, width), lambda g: (0, g)),
+        compiler_params=pltpu.CompilerParams(vmem_limit_bytes=48 * 2**20),
+        name="times_folded",
+    )(rows_in, weights)
+
+
+def expand_back_kernel(x_ref, w_ref, o_ref):
+    weight = w_ref[...].reshape(o_ref.shape[1], w_ref.shape[2])
+
+    @pl.when(pl.program_id(0) == 0)
+    def _():
+        o_ref[...] = jnp.zeros_like(o_ref)
+
+    o_ref[...] += contract(x_ref[...], weight, 1, 1)
+
+
+def times_folded_back(rows_in, weights, fold, at, width):
+    m = rows_in.shape[0]
+    k = weights.shape[0] * fold
+    groups = weights.shape[1] // fold
+    return pl.pallas_call(
+        expand_back_kernel,
+        grid=(groups,),
+        out_shape=jax.ShapeDtypeStruct((m, k), jnp.float32),
+        in_specs=[
+            pl.BlockSpec((m, width), lambda g: (0, g)),
+            pl.BlockSpec((weights.shape[0], fold, width), lambda g: (0, g, at)),
+        ],
+        out_specs=pl.BlockSpec((m, k), lambda g: (0, 0)),
+        compiler_params=pltpu.CompilerParams(vmem_limit_bytes=48 * 2**20),
+        name="times_folded_back",
+    )(rows_in, weights)
+
+
+def grads_kernel(
+    tile, n_q, n_e, n_o, fold, normed_ref, dq_ref, full_ref, dexp_ref, att_ref, dattn_ref, dlat_ref, gain_ref, o_ref
+):
+    t = pl.program_id(0)
+    n_dev, rows, _ = o_ref.shape
+    t_q, t_e, t_o = n_q // tile, n_e // tile, n_o // tile
+
+    def cut(ref, i):
+        return ref[:, pl.ds(pl.multiple_of(i * tile, tile), tile)]
+
+    def put(left, right):
+        done = jnp.dot(left, right, preferred_element_type=jnp.float32).astype(o_ref.dtype)
+        return done.reshape(n_dev, done.shape[0] // n_dev, tile)
+
+    @pl.when(t < t_q)
+    def _():
+        o_ref[...] = put(normed_ref[...], cut(dq_ref, t))
+
+    @pl.when((t >= t_q) & (t < t_q + t_e))
+    def _():
+        for g in range(rows // fold):
+            part = cut(dexp_ref, g * t_e + t - t_q)
+            o_ref[:, g * fold : (g + 1) * fold, :] = put(full_ref[...], part)
+
+    @pl.when((t >= t_q + t_e) & (t < t_q + t_e + t_o))
+    def _():
+        o_ref[...] = put(att_ref[...], cut(dattn_ref, t - t_q - t_e))
+
+    @pl.when(t >= t_q + t_e + t_o)
+    def _():
+        i = t - t_q - t_e - t_o
+        o_ref[...] = put(normed_ref[...], cut(dlat_ref, i)) + cut_gain(gain_ref, i, tile)
+
+
+def cut_gain(ref, i, tile):
+    return ref[:, :, pl.ds(pl.multiple_of(i * tile, tile), tile)]
+
+
+def packed_grads(n_dev, rows, fold, normed, dq, full, dexp, att, dattn, dlat, gain):
+    tile = 256
+    n_q, n_e, n_o, n_l = dq.shape[1], dexp.shape[1] // (rows // fold), dattn.shape[1], dlat.shape[1]
+    cols = n_q + n_e + n_o + n_l
+    whole = lambda a: pl.BlockSpec(a.shape, lambda i: (0,) * a.ndim)
+    operands = (normed, dq, full, dexp, att, dattn, dlat, gain)
+    return pl.pallas_call(
+        functools.partial(grads_kernel, tile, n_q, n_e, n_o, fold),
+        grid=(cols // tile,),
+        out_shape=jax.ShapeDtypeStruct((n_dev, rows, cols), jnp.bfloat16),
+        in_specs=[whole(a) for a in operands],
+        out_specs=pl.BlockSpec((n_dev, rows, tile), lambda i: (0, 0, i)),
+        compiler_params=pltpu.CompilerParams(vmem_limit_bytes=56 * 2**20),
+        name="packed_grads",
+    )(*operands)
+
+
+def picks(pick_ref, share_ref):
+    pairs, slots, toks = pick_ref.shape
+    found = []
+    for p in range(pairs):
+        pick = pick_ref[p]
+        scale = jnp.sum(pick.astype(jnp.float32) * share_ref[p], axis=1, keepdims=True)
+        r, t = slice(p * slots, (p + 1) * slots), slice(p * toks, (p + 1) * toks)
+        found.append((pick, r, t, scale))
+    return found
+
+
+def forward_kernel(
+    x_ref, pick_ref, share_ref, wg_ref, wu_ref, wd_ref, ws_ref, wsd_ref,
+    out_ref, rows_ref, pre_ref, lift_ref, hid_ref, both_ref, hs_ref,
+):
+    f32, bf = jnp.float32, out_ref.dtype
+    found = picks(pick_ref, share_ref)
+    for pick, r, t, _ in found:
+        rows_ref[r, :] = jnp.dot(pick, x_ref[t, :], preferred_element_type=f32).astype(bf)
+    pre = contract(rows_ref[...], wg_ref[...], 1, 1)
+    lift = contract(rows_ref[...], wu_ref[...], 1, 1)
+    hidden = (pre / (1.0 + jnp.exp(-pre)) * lift).astype(bf)
+    pre_ref[...] = pre
+    lift_ref[...] = lift
+    hid_ref[...] = hidden
+    scale = jnp.concatenate([item[3] for item in found], axis=0)
+    done = (jnp.dot(hidden, wd_ref[...], preferred_element_type=f32) * scale).astype(bf)
+    lanes = wsd_ref.shape[0]
+    both = jnp.dot(x_ref[...], ws_ref[...], preferred_element_type=f32)
+    both_ref[...] = both
+    pre, lift = both[:, :lanes], both[:, lanes:]
+    hs_ref[...] = (pre / (1.0 + jnp.exp(-pre)) * lift).astype(bf)
+    for pick, r, t, _ in found:
+        shared = jnp.dot(hs_ref[t, :], wsd_ref[...], preferred_element_type=f32)
+        out_ref[t, :] = (contract(pick, done[r, :], 0, 0) + shared).astype(bf)
+
+
+def backward_kernel(
+    c_ref, pick_ref, share_ref, pre_ref, lift_ref, both_ref, wg_ref, wu_ref, wd_ref, ws_ref, wsd_ref,
+    dx_ref, drows_ref, dpre_ref, dlift_ref, dsh_ref,
+):
+    f32, bf = jnp.float32, dx_ref.dtype
+    found = picks(pick_ref, share_ref)
+
+    def gates(pre, lift, d_hidden):
+        sigma = 1.0 / (1.0 + jnp.exp(-pre))
+        d_pre = (d_hidden * lift * (sigma * (1.0 + pre * (1.0 - sigma)))).astype(bf)
+        return d_pre, (d_hidden * (pre * sigma)).astype(bf)
+
+    for pick, r, t, scale in found:
+        taken = jnp.dot(pick, c_ref[t, :], preferred_element_type=f32)
+        drows_ref[r, :] = (taken * scale).astype(bf)
+    d_hidden = contract(drows_ref[...], wd_ref[...], 1, 1)
+    d_pre, d_lift = gates(pre_ref[...], lift_ref[...], d_hidden)
+    dpre_ref[...] = d_pre
+    dlift_ref[...] = d_lift
+    d_done = (contract(d_pre, wg_ref[...], 1, 0) + contract(d_lift, wu_ref[...], 1, 0)).astype(bf)
+    lanes = wsd_ref.shape[0]
+    d_shared = contract(c_ref[...], wsd_ref[...], 1, 1)
+    d_pre, d_lift = gates(both_ref[:, :lanes], both_ref[:, lanes:], d_shared)
+    dsh_ref[:, :lanes] = d_pre
+    dsh_ref[:, lanes:] = d_lift
+    for pick, r, t, _ in found:
+        shared = contract(dsh_ref[t, :], ws_ref[...], 1, 1)
+        dx_ref[t, :] = (contract(pick, d_done[r, :], 0, 0) + shared).astype(bf)
+
+
+def by_tiles(kernel, name, micros, moving, fixed, outs, steps):
+    def tile(shape):
+        cut = (shape[0] // steps,) + tuple(shape[1:])
+        return pl.BlockSpec(cut, lambda i: (i,) + (0,) * (len(shape) - 1))
+
+    keep = lambda a: pl.BlockSpec(a.shape, lambda i: (0,) * a.ndim, pipeline_mode=pl.Buffered(1))
+    return pl.pallas_call(
+        kernel,
+        grid=(steps,),
+        out_shape=tuple(jax.ShapeDtypeStruct(s, d) for s, d in outs),
+        in_specs=[tile(a.shape) for a in moving] + [keep(a) for a in fixed],
+        out_specs=tuple(tile(s) for s, d in outs),
+        compiler_params=pltpu.CompilerParams(vmem_limit_bytes=62 * 2**20),
+        cost_estimate=busy(micros),
+        name=name,
+    )(*moving, *fixed)
 
 
 def norm_back(values, gain, upstream):
@@ -431,39 +1041,53 @@
         ),
         axis=0,
     )
-    info = jnp.concatenate([by_expert, jnp.sum(levels, axis=1)[None]], axis=0).astype(bf)
-    info = jnp.pad(info, ((0, rows - info.shape[0]), (0, 0)))
+    line = lambda v: jnp.pad(v, (0, toks - v.shape[0]))[None]
+    info = jnp.concatenate(
+        [
+            by_expert.astype(bf),
+            jnp.sum(levels, axis=1).astype(bf)[None],
+            line(norm_gain),
+            line(mixer_gain),
+            line(latent_gain),
+            jnp.zeros((rows - experts_count - 4, toks), bf),
+        ],
+        axis=0,
+    )
     folded = jnp.concatenate(jnp.split(expand_proj, groups, axis=1), axis=0)
-    gains = jnp.stack([norm_gain, mixer_gain, jnp.pad(latent_gain, (0, rows - latent_rows))], axis=1)
-    gains = jnp.pad(gains, ((0, 0), (0, 64 - 3)))
-    packed = jnp.concatenate([query_proj, output_proj, latent_proj, gains, folded, info], axis=1)
-    spots = [0]
-    for part in (n_q, n_o, n_l, 64, n_e, toks):
-        spots.append(spots[-1] + part)
-    weights = gather_all(packed, 1)
-    w_query = weights[:, :, : spots[1]].reshape(width, n_q)
-    w_output = weights[:, :, spots[1] : spots[2]].reshape(width, n_o)
-    w_latent = weights[:, :, spots[2] : spots[3]].reshape(width, n_l)
-    all_gains = weights[:, :, spots[3] : spots[4]].astype(f32)
-    gain_one = all_gains[:, :, 0].reshape(-1)
-    gain_two = all_gains[:, :, 1].reshape(-1)
-    gain_latent = all_gains[:, :latent_rows, 2].reshape(-1)
-    w_expand = weights[:, :, spots[4] : spots[5]].reshape(n_dev, groups, latent_rows, n_e)
-    w_expand = jnp.swapaxes(w_expand, 1, 2).reshape(KVL, groups * n_e)
-    all_info = weights[:, :, spots[5] :].astype(f32)
+    aside = n_q + n_e + n_o + 5 * toks
+    packed = jnp.concatenate(
+        [
+            query_proj,
+            folded,
+            output_proj,
+            jnp.pad(latent_proj, ((0, 0), (0, 5 * toks - n_l))),
+            info,
+            jnp.zeros((rows, 2 * toks), bf),
+        ],
+        axis=1,
+    )
+    grouped = gather_all(packed, 1)
+    grouped, held_cotangent = lax.optimization_barrier((grouped, cotangent[0]))
+    all_info = grouped[:, :, :, aside : aside + toks].astype(f32).reshape(n_dev, rows, toks)
+    gain_one = all_info[:, experts_count + 1, :rows].reshape(-1)
+    gain_two = all_info[:, experts_count + 2, :rows].reshape(-1)
+    gain_latent = all_info[:, experts_count + 3, :latent_rows].reshape(-1)
+    blocks = grouped.reshape(n_dev, rows, -1)
+    weights = blocks.reshape(width, -1)
 
     n_s = shared_down.shape[0]
-    fill = jnp.zeros((rows, n_dev, 256 - 2 * n_s), bf)
-    gate_up = jnp.concatenate(
-        [shared_gate.reshape(rows, n_dev, n_s), shared_up.reshape(rows, n_dev, n_s), fill], axis=2
-    )
-    w_shared = spread_all(jnp.swapaxes(gate_up, 0, 1), 11).reshape(width, -1)[:, : 2 * n_s]
-
-    cot_all = gather_all(cotangent[0], 3).reshape(-1, width)
+    lanes = 128
+    fill = lambda v: jnp.pad(v.reshape(rows, n_dev, n_s), ((0, 0), (0, 0), (0, lanes - n_s)))
+    gate_up = jnp.concatenate([fill(shared_gate), fill(shared_up)], axis=2)
+    w_shared = lax.all_to_all(
+        jnp.swapaxes(gate_up, 0, 1), both, split_axis=0, concat_axis=0, tiled=True
+    ).reshape(width, 2 * lanes)
+
+    cot_all = lax.all_gather(held_cotangent, both, axis=0, tiled=True)
 
     normed = norm_apply(inputs, gain_one).astype(bf)
-    query_raw = jnp.dot(normed, w_query, preferred_element_type=f32).reshape(toks, H, DN + DR)
-    latent_raw = jnp.dot(normed, w_latent, preferred_element_type=f32)
+    query_raw = times_columns(normed, weights, 0, n_q // 512, 512).reshape(toks, H, DN + DR)
+    latent_raw = times_columns(normed, weights, (n_q + n_e + n_o) // 512, 2, 512)[:, :n_l]
     latent = latent_raw[:, :KVL]
     latent_normed = norm_apply(latent, gain_latent).astype(bf)
     positions = seq * toks + jnp.arange(toks, dtype=jnp.int32)
@@ -478,7 +1102,7 @@
     pair = jnp.where(seq == 0, pair, pair[::-1]).reshape(2 * toks, -1)
     latent_full = pair[:, :KVL]
     rotary_full = pair[:, KVL : KVL + DR]
-    expanded = jnp.dot(latent_full, w_expand, preferred_element_type=f32).astype(bf)
+    expanded = times_folded(latent_full, blocks, latent_rows, n_q // n_e, n_e)
     expanded = expanded.reshape(2 * toks, H, DN + DV)
     keys, values = expanded[:, :, :DN], expanded[:, :, DN:]
     keys = jnp.concatenate(
@@ -498,8 +1122,8 @@
     soft_low = soft.astype(bf)
     mixed = jnp.einsum("hqk,khd->qhd", soft_low, values, preferred_element_type=f32).astype(bf)
     attended = mixed.reshape(toks, H * DV)
-    middle = inputs + jnp.dot(attended, w_output, preferred_element_type=f32)
-    normed_two = pass_on(norm_apply(middle, gain_two).astype(bf))
+    middle = inputs + times_columns(attended, weights, (n_q + n_e) // 512, n_o // 512, 512)
+    normed_two = norm_apply(middle, gain_two).astype(bf)
 
     gathered = gather_all(normed_two, 5)
     x_all = gathered.reshape(-1, width)
@@ -507,66 +1131,86 @@
     mask = level > 0
     share = level / all_info[:, experts_count]
     slot = jnp.cumsum(mask.astype(jnp.int32), axis=1) - 1
-    pick = mask[:, None, :] & (
-        slot[:, None, :] == jnp.arange(capacity, dtype=jnp.int32)[None, :, None]
-    )
-    share_rows = jnp.sum(jnp.where(pick, share[:, None, :], 0.0), axis=2)
+    pair = lambda v: v.reshape(n_dev // 2, 2 * toks)
+    slot = pair(slot + capacity * (jnp.arange(n_dev, dtype=jnp.int32)[:, None] % 2))
+    pick = pair(mask)[:, None, :] & (
+        slot[:, None, :] == jnp.arange(2 * capacity, dtype=jnp.int32)[None, :, None]
+    )
     pick = pick.astype(bf)
-    expert_rows = jnp.einsum("bst,btd->bsd", pick, gathered, preferred_element_type=f32)
-    expert_rows = expert_rows.astype(bf).reshape(n_dev * capacity, width)
-    gate_weight, up_weight, down_weight = expert_gate[0], expert_up[0], expert_down[0]
-    n_h = gate_weight.shape[1]
-    expert_pre = jnp.dot(expert_rows, gate_weight, preferred_element_type=f32)
-    expert_lift = jnp.dot(expert_rows, up_weight, preferred_element_type=f32)
-    expert_hidden = (sigmoid_linear(expert_pre) * expert_lift).astype(bf)
-    shared_both = jnp.dot(x_all, w_shared, preferred_element_type=f32)
-    shared_pre, shared_lift = shared_both[:, :n_s], shared_both[:, n_s:]
-    shared_hidden = (sigmoid_linear(shared_pre) * shared_lift).astype(bf)
-    spread = jnp.einsum(
-        "bst,bsd->btd",
-        pick,
-        expert_hidden.reshape(n_dev, capacity, n_h),
-        preferred_element_type=f32,
-    )
-    spread = (spread * share[:, :, None]).astype(bf).reshape(-1, n_h)
-    hidden_all = jnp.concatenate([spread, shared_hidden], axis=1)
-    down_all = jnp.concatenate([down_weight, shared_down], axis=0)
-    out_parts = jnp.dot(hidden_all, down_all, preferred_element_type=f32).astype(bf)
-    layer_out = middle + scatter_sum(out_parts.reshape(n_dev, toks, width), 6)
-
+    pair_share = pair(share)[:, None, :]
+    weights_here = (
+        expert_gate[0].T,
+        expert_up[0].T,
+        expert_down[0],
+        w_shared,
+        jnp.pad(shared_down, ((0, lanes - n_s), (0, 0))),
+    )
+    n_rows, n_h, steps = n_dev * capacity, expert_gate.shape[2], n_dev // 4
+    out_parts, e_rows, e_pre, e_lift, e_hidden, s_both, s_hidden = by_tiles(
+        forward_kernel,
+        "experts_forward",
+        40,
+        (x_all, pick, pair_share),
+        weights_here,
+        (
+            ((n_dev * toks, width), bf),
+            ((n_rows, width), bf),
+            ((n_rows, n_h), f32),
+            ((n_rows, n_h), f32),
+            ((n_rows, n_h), bf),
+            ((n_dev * toks, 2 * lanes), f32),
+            ((n_dev * toks, lanes), bf),
+        ),
+        steps,
+    )
+    layer_out = middle + lax.psum_scatter(
+        out_parts, both, scatter_dimension=0, tiled=True
+    ).astype(f32)
     grad_out = cotangent[0].astype(f32)
-    d_rows = jnp.einsum(
-        "bst,btd->bsd", pick, cot_all.reshape(n_dev, toks, width), preferred_element_type=f32
-    )
-    d_rows = (d_rows * share_rows[:, :, None]).astype(bf).reshape(n_dev * capacity, width)
-    expert_down_grad = contract(expert_hidden, d_rows, 0, 0)
-    d_hidden = contract(d_rows, down_weight, 1, 1)
-    d_pre = (d_hidden * expert_lift * silu_slope(expert_pre)).astype(bf)
-    d_lift = (d_hidden * sigmoid_linear(expert_pre)).astype(bf)
-    expert_gate_grad = contract(expert_rows, d_pre, 0, 0)
-    expert_up_grad = contract(expert_rows, d_lift, 0, 0)
-    d_x = contract(d_pre, gate_weight, 1, 1) + contract(d_lift, up_weight, 1, 1)
-    d_x = d_x.astype(bf).reshape(n_dev, capacity, width)
-    d_x = jnp.einsum("bst,bsd->btd", pick, d_x, preferred_element_type=f32).reshape(-1, width)
-    shared_down_grad = contract(shared_hidden, cot_all, 0, 0)
-    d_shared_hidden = contract(cot_all, shared_down, 1, 1)
-    d_shared_pre = (d_shared_hidden * shared_lift * silu_slope(shared_pre)).astype(bf)
-    d_shared_lift = (d_shared_hidden * sigmoid_linear(shared_pre)).astype(bf)
-    d_shared_both = jnp.concatenate([d_shared_pre, d_shared_lift], axis=1)
-    shared_both_grad = contract(x_all, d_shared_both, 0, 0).astype(bf)
-    d_x = (d_x + contract(d_shared_both, w_shared, 1, 1)).astype(bf)
-    d_normed_two = scatter_sum(d_x.reshape(n_dev, toks, width), 7)
-    shared_both_grad = jnp.pad(shared_both_grad, ((0, 0), (0, 256 - 2 * n_s)))
-    shared_back = spread_all(shared_both_grad.reshape(n_dev, rows, 256), 12)
+    d_parts, d_rows, d_pre, d_lift, d_shared = by_tiles(
+        backward_kernel,
+        "experts_backward",
+        50,
+        (cot_all, pick, pair_share, e_pre, e_lift, s_both),
+        weights_here,
+        (
+            ((n_dev * toks, width), bf),
+            ((n_rows, width), bf),
+            ((n_rows, n_h), bf),
+            ((n_rows, n_h), bf),
+            ((n_dev * toks, 2 * lanes), bf),
+        ),
+        steps,
+    )
+    expert_down_grad = contract(e_hidden, d_rows, 0, 0)
+    expert_gate_grad = contract(e_rows, d_pre, 0, 0)
+    expert_up_grad = contract(e_rows, d_lift, 0, 0)
+    shared_down_grad = contract(s_hidden, cot_all, 0, 0)[:n_s]
+    shared_both_grad = contract(x_all, d_shared, 0, 0).astype(bf)
+    expert_down_grad, expert_gate_grad, expert_up_grad, shared_down_grad, shared_both_grad, d_parts = (
+        lax.optimization_barrier(
+            (
+                expert_down_grad,
+                expert_gate_grad,
+                expert_up_grad,
+                shared_down_grad,
+                shared_both_grad,
+                d_parts,
+            )
+        )
+    )
+    d_normed_two = scatter_sum(d_parts.reshape(n_dev, toks, width), 7)
+    shared_back = lax.all_to_all(
+        shared_both_grad.reshape(n_dev, rows, 256), both, split_axis=0, concat_axis=0, tiled=True
+    )
     shared_back = jnp.swapaxes(shared_back, 0, 1).astype(f32)
     shared_gate_grad = shared_back[:, :, :n_s].reshape(rows, n_dev * n_s)
-    shared_up_grad = shared_back[:, :, n_s : 2 * n_s].reshape(rows, n_dev * n_s)
+    shared_up_grad = shared_back[:, :, lanes : lanes + n_s].reshape(rows, n_dev * n_s)
 
     d_middle_norm, mixer_gain_grad = norm_back(middle, gain_two, d_normed_two)
     d_middle = grad_out + d_middle_norm
     d_attn = d_middle.astype(bf)
-    output_proj_grad = contract(attended, d_attn, 0, 0)
-    d_mixed = contract(d_attn, w_output, 1, 1).astype(bf).reshape(toks, H, DV)
+    d_mixed = times_rows(d_attn, weights, (n_q + n_e) // n_o, n_o, 512).astype(bf).reshape(toks, H, DV)
     d_soft = jnp.einsum("qhd,khd->hqk", d_mixed, values, preferred_element_type=f32)
     delta = jnp.sum(soft * d_soft, axis=-1, keepdims=True)
     d_scores = (soft * (d_soft - delta)).astype(bf)
@@ -588,11 +1232,9 @@
         .astype(bf)
         .reshape(toks, -1)
     )
-    query_proj_grad = contract(normed, d_query_raw, 0, 0)
     d_expanded = jnp.concatenate([d_keys[:, :, :DN].astype(bf), d_values], axis=2)
     d_expanded = d_expanded.reshape(2 * toks, -1)
-    expand_proj_grad = contract(latent_full, d_expanded, 0, 0)
-    d_latent_pair = contract(d_expanded, w_expand, 1, 1)
+    d_latent_pair = times_folded_back(d_expanded, blocks, latent_rows, n_q // n_e, n_e)
     d_rotary_pair = jnp.sum(d_keys[:, :, DN:], axis=1)
     d_pair = jnp.concatenate(
         [d_latent_pair, d_rotary_pair, jnp.zeros((2 * toks, 64), f32)], axis=1
@@ -602,13 +1244,13 @@
     d_key_rotary = rotate(d_pair[:, KVL : KVL + DR], cosine, -sine)
     d_latent, latent_gain_grad = norm_back(latent, gain_latent, d_latent_normed)
     d_latent_raw = jnp.concatenate([d_latent, d_key_rotary], axis=1).astype(bf)
-    latent_proj_grad = contract(normed, d_latent_raw, 0, 0)
-    d_normed = contract(d_query_raw, w_query, 1, 1) + contract(d_latent_raw, w_latent, 1, 1)
+    d_latent_wide = jnp.pad(d_latent_raw, ((0, 0), (0, 1024 - n_l)))
+    d_normed = times_rows(d_query_raw, weights, 0, n_q, 512) + times_rows(
+        d_latent_wide, weights, (n_q + n_e + n_o) // 1024, 1024, 512
+    )
     d_inputs, norm_gain_grad = norm_back(inputs, gain_one, d_normed)
     input_grad = d_middle + d_inputs
 
-    folded_grad = expand_proj_grad.astype(bf).reshape(n_dev, latent_rows, groups, n_e)
-    folded_grad = jnp.swapaxes(folded_grad, 1, 2).reshape(n_dev, rows, n_e)
     latent_gain_part = jnp.pad(
         latent_gain_grad.reshape(n_dev, latent_rows), ((0, 0), (0, rows - latent_rows))
     )
@@ -620,23 +1262,27 @@
         ],
         axis=2,
     )
-    gain_parts = jnp.pad(gain_parts, ((0, 0), (0, 0), (0, 64 - 3))).astype(bf)
-    out_parts_grad = output_proj_grad.astype(bf).reshape(n_dev, rows, n_o)
-    output_grad = scatter_sum(out_parts_grad, 9)
-    grad_parts = jnp.concatenate(
-        [
-            query_proj_grad.astype(bf).reshape(n_dev, rows, n_q),
-            folded_grad,
-            latent_proj_grad.astype(bf).reshape(n_dev, rows, n_l),
-            gain_parts,
-        ],
-        axis=2,
-    )
-    grads = scatter_sum(grad_parts, 10)
-    at_latent = n_q + n_e
+    wide = 768
+    gain_parts = jnp.pad(gain_parts, ((0, 0), (0, 0), (n_l, wide - n_l - 3))).astype(bf)
+    grad_parts = packed_grads(
+        n_dev,
+        rows,
+        latent_rows,
+        normed.T,
+        d_query_raw,
+        latent_full.T,
+        d_expanded,
+        attended.T,
+        d_attn,
+        d_latent_wide[:, :wide],
+        gain_parts,
+    )
+    grads = scatter_sum(grad_parts, 9)
+    at_output = n_q + n_e
+    at_latent = at_output + n_o
     at_gain = at_latent + n_l
     expand_out = jnp.concatenate(
-        jnp.split(grads[:, n_q:at_latent], groups, axis=0), axis=1
+        jnp.split(grads[:, n_q:at_output], groups, axis=0), axis=1
     )
     return (
         layer_out[None],
@@ -646,7 +1292,7 @@
         grads[:, at_latent:at_gain],
         grads[:latent_rows, at_gain + 2],
         expand_out,
-        output_grad,
+        grads[:, at_output:at_latent],
         grads[:, at_gain + 1],
         shared_gate_grad,
         shared_up_grad,

time: 1330 us -> 908 us (0.68)
  waiting for transfers between devices: 805 us -> 0.04 us
  Pallas kernels: 1.88 us -> 716 us
  matrix products: 296 us -> 60.3 us
  local copies, waits for them, and re-layouts: 164 us -> 63.3 us
    pallas_call x1 -> x17, Pallas kernels: 1.88 us -> 716 us  [the longest x2 279 us: scatter_sum(): pl.pallas_call(functools.partial(rs_kernel, rows // 16), out_shape=jax.Sh...]
    reduce_scatter x4 -> x1, waiting for transfers between devices: 528 us -> 0.01 us  [block_body(): lax.psum_scatter(out_parts, both, scatter_dimension=0, tiled=True)]
    all_gather x3 -> x1, waiting for transfers between devices: 276 us -> 0.01 us  [block_body(): cot_all = lax.all_gather(held_cotangent, both, axis=0, tiled=True)]
    dot_general x12 -> x0, matrix products: 127 us -> none  [the longest x1 24.5 us: block_body(): jnp.dot(hidden_all, down_all, preferred_element_type=f32).astype(bf)]
    dot_general x18 -> x5, matrix products: 158 us -> 46.8 us  [contract(): lax.dot_general(left, right, (((left_dim,), (right_dim,)), ((), ())), pre...]
    concatenate x3 -> x2, local copies, waits for them, and re-layouts: 30.7 us -> 0.22 us  [the longest x1 0.22 us: block_body(): jnp.concatenate([by_expert.astype(bf), jnp.sum(levels, axis=1).astype(bf)...]
    slice x9, local copies, waits for them, and re-layouts: 32.7 us -> 6.85 us  [the longest x1 1.87 us: block_body(): grads[:, at_output:at_latent]]
    dot_general x1 -> x0, local copies, waits for them, and re-layouts: 16.7 us -> none  [block_body(): jnp.dot(normed, w_query, preferred_element_type=f32)]
  transfers between devices with their start and end apart: 11 -> 4, of which waited for: 5 -> 0; matrix products, arithmetic and copies ran while one was open for 32% -> 15% of each run, Pallas kernels for 0% -> 66%
where the time goes in v2:
time: 908 us; the launch traced here: 893 us
  Pallas kernels  716 us (79%)
  local copies, waits for them, and re-layouts  63.3 us (7%)
  matrix products  60.3 us (7%)
  other arithmetic  27.9 us (3%)
  between operations  15.7 us (2%)
  starting transfers between devices  9.43 us (1%)
    pallas_call x2, Pallas kernels, scatter_sum(): pl.pallas_call(functools.partial(rs_kernel, rows // 16), out_shape=jax.Sh...  279 us
    pallas_call x2, Pallas kernels, gather_all(): pl.pallas_call(functools.partial(ag_kernel, rows // 16), out_shape=jax.Sh...  232 us
    pallas_call x2, Pallas kernels, by_tiles(): pl.pallas_call(kernel, grid=(steps,), out_shape=tuple((jax.ShapeDtypeStru...  119 us
    dot_general x5, matrix products, contract(): lax.dot_general(left, right, (((left_dim,), (right_dim,)), ((), ())), pre...  46.8 us
    pallas_call x1, Pallas kernels, packed_grads(): pl.pallas_call(functools.partial(grads_kernel, tile, n_q, n_e, n_o, fold)...  24.4 us
    pallas_call x2, Pallas kernels, seq_swap(): pl.pallas_call(swap_kernel, out_shape=jax.ShapeDtypeStruct(grouped, piece...  20.7 us
  transfers between devices with their start and end apart: 4, of which 0 were waited for; matrix products, arithmetic and copies ran while one was open for 15% of the time, Pallas kernels for 66%

profile of v2, /device:TPU:0, one launch (start us, length us, event | category | flops | bytes accessed | tf_op | source)
XLA Modules:
  0.0 893.0 jit_solution(6528634767854198635)
XLA Ops:
  15.0 128.1 %gather_rows.2 = bf16[32,8,8,7168]{3,2,1,0:T(8,128)(2,1)} custom-call(bf16[8,8,7168]{2,1,0:T(8,128)(2,1)} %bitcast.182), custom_call_target="tpu_custom_call" | custom-call | bytes 471408000 | tf_op jit(solution)/shard_map/gather_rows/pallas_call | solution.py:501
  147.4 3.9 all-to-all-start
  154.6 2.7 times_columns.3
  157.4 7.4 times_columns.4
  170.7 7.8 seq_swap.2
  186.5 4.0 times_folded.1
  197.7 3.9 fusion.73
  203.1 2.9 convolution_convert_fusion.2
  207.3 4.9 times_columns.5
  213.6 103.9 %gather_rows.3 = bf16[32,16,8,2048]{3,2,1,0:T(8,128)(2,1)} custom-call(bf16[16,8,2048]{2,1,0:T(8,128)(2,1)} %fusion.28.x_ref), custom_call_target="tpu_custom_call" | custom-call | bytes 299376000 | tf_op jit(solution)/shard_map/gather_rows/pallas_call | solution.py:501
  319.2 54.9 %experts_forward.1 = (bf16[4096,2048]{1,0:T(8,128)(2,1)}, bf16[2304,2048]{1,0:T(8,128)(2,1)}, f32[2304,704]{1,0:T(8,128)}, f32[2304,704]{1,0:T(8,128)}, bf16[230...) custom-call(bf16[4096,2048]{1,0:T(8,128)(2,1)} %bitcast.152, ...), custom_call_target="tpu_custom_call" | custom-call | bytes 140000000 | tf_op jit(solution)/shard_map/experts_forward/pallas_call | solution.py:982
  376.6 64.0 %experts_backward.1 = (bf16[4096,2048]{1,0:T(8,128)(2,1)}, bf16[2304,2048]{1,0:T(8,128)(2,1)}, bf16[2304,704]{1,0:T(8,128)(2,1)}, bf16[2304,704]{1,0:T(8,128)(2,1)}, bf16[4096,256]{1,0:T(8,128)(2,1)}) custom-call(bf16[4096,2048]{1,0:T(8,128)(2,1)} %all-gather.2.cloned.1.call-done.c_ref, bf16[16,144,256]{2,1,0:T(8,128)(2,1)} %fusion.2.pick_ref, ...), custom_call_target="tpu_custom_call" | custom-call | bytes 175000000 | tf_op jit(solution)/shard_map/experts_backward/pallas_call | solution.py:982
  440.6 10.1 %fusion.19 = f32[88,2048]{1,0:T(8,128)} fusion(bf16[4096,2048]{1,0:T(8,128)(2,1)} %all-gather.2.cloned.1.call-done.c_ref, bf16[4096,128]{1,0:T(8,128)(2,1)} %get-tuple-element.46), kind=kOutput, calls=%fused_computation.45 | convolution fusion | flops 1476395008 | bytes 18546688 | tf_op jit(solution)/shard_map/dot_general | solution.py:49
  450.8 9.8 %convolution_convert_fusion = bf16[2048,256]{1,0:T(8,128)(2,1)} fusion(bf16[4096,2048]{1,0:T(8,128)(2,1)} %bitcast.153, bf16[4096,256]{1,0:T(8,128)(2,1)S(1)} %copy-done.60), kind=kOutput, calls=%fused_computation.2 | convolution fusion | flops 4295491584 | bytes 19922944 | tf_op jit(solution)/shard_map/dot_general | solution.py:49
  460.6 8.9 fusion.74
  469.6 9.0 %fusion.75 = f32[2048,704]{0,1:T(8,128)} fusion(bf16[2304,2048]{1,0:T(8,128)(2,1)S(1)} %bitcast.200, bf16[2304,704]{1,0:T(8,128)(2,1)S(1)} %copy-done.59), kind=kOutput, calls=%fused_computation.169 | convolution fusion | flops 6643777536 | bytes 18448384 | tf_op jit(solution)/shard_map/dot_general | solution.py:49
  478.6 9.0 %fusion.76 = f32[2048,704]{0,1:T(8,128)} fusion(bf16[2304,2048]{1,0:T(8,128)(2,1)S(1)} %bitcast.200, bf16[2304,704]{1,0:T(8,128)(2,1)S(1)} %copy-done.58), kind=kOutput, calls=%fused_computation.170 | convolution fusion | flops 6643777536 | bytes 18448384 | tf_op jit(solution)/shard_map/dot_general | solution.py:49
  487.6 145.0 %scatter_sum.2 = f32[16,8,2048]{2,1,0:T(8,128)} custom-call(bf16[32,16,8,2048]{3,2,1,0:T(8,128)(2,1)} %bitcast.154), custom_call_target="tpu_custom_call" | custom-call | bytes 299376000 | tf_op jit(solution)/shard_map/scatter_sum/pallas_call | solution.py:649
  632.6 5.5 all-to-all-start.1
  640.2 6.1 times_rows.3
  647.9 2.6 multiply_reduce_fusion
  656.3 2.9 copy.164.x_ref.dexp_ref
  661.4 4.3 times_folded_back.1
  666.7 12.9 %seq_swap.3 = f32[2,16,8,640]{3,2,1,0:T(8,128)} custom-call(f32[2,16,8,640]{3,2,1,0:T(8,128)} %bitcast.179), custom_call_target="tpu_custom_call" | custom-call | bytes 28000000 | tf_op jit(solution)/shard_map/seq_swap/pallas_call | solution.py:748
  681.5 3.0 multiply_bitcast_fusion.1
  685.3 4.1 times_rows.5
  692.4 7.8 times_rows.4
  703.5 24.4 %packed_grads.1 = bf16[32,64,6912]{2,1,0:T(8,128)(2,1)} custom-call(bf16[2048,128]{1,0:T(8,128)(2,1)} %copy.159.normed_ref, bf16[128,3072]{1,0:T(8,128)(2,1)} %copy-done.1, bf16[512,256]{1,0:T(8,128)(2,1)} %get-tuple-element.87.full_ref, bf16[256,4096]{1,0:T(8,128)(2,1)} %copy-done, bf16[2048,128]{1,0:T(8,128)(2,1)} %bitcast.181, ...), custom_call_target="tpu_custom_call" | custom-call | tf_op jit(solution)/shard_map/packed_grads/pallas_call | solution.py:898
  727.9 133.9 %scatter_sum.3 = f32[8,8,6912]{2,1,0:T(8,128)} custom-call(bf16[32,8,8,6912]{3,2,1,0:T(8,128)(2,1)} %bitcast.151), custom_call_target="tpu_custom_call" | custom-call | bytes 457072000 | tf_op jit(solution)/shard_map/scatter_sum/pallas_call | solution.py:649
  876.7 2.9 copy.161
  879.6 2.7 reshape.431
  882.2 3.5 fusion.14
  (271 shorter events, 80.5 us)
Async XLA Ops:
  7.2 369.5 %all-gather.2.cloned.1.call-start = ((), (), s32[]{:S(2)}) async-start(), calls=%async_computation.4 | async-start | bytes 17301504 | tf_op jit(solution)/shard_map/all_gather | solution.py:1086
  15.0 128.2 %copy-start.23 = (bf16[64,2816]{1,0:T(8,128)(2,1)S(1)}, bf16[64,2816]{1,0:T(8,128)(2,1)}, u32[]{:S(2)}) copy-start(bf16[64,2816]{1,0:T(8,128)(2,1)} %param.26) | copy-start | bytes 1081348
  147.4 171.8 %all-to-all-start = ((bf16[32,64,256]{2,1,0:T(8,128)(2,1)}), bf16[32,64,256]{2,1,0:T(8,128)(2,1)}, u32[]{:S(2)}, u32[]{:S(2)}) async-start(bf16[32,64,256]{2,1,0:T(8,128)(2,1)} %fusion.16), calls=%async_computation | async-start | bytes 2097152 | tf_op jit(solution)/shard_map/all_to_all | solution.py:1082
  151.2 731.0 %reduce-scatter.2.cloned.1.call-start = ((), (), s32[]{:S(2)}) async-start(), calls=%async_computation.3 | async-start | bytes 17301504 | tf_op jit(solution)/shard_map/reduce_scatter | solution.py:1166
  157.4 12.4 %copy-start.2 = (f32[128,1024]{1,0:T(8,128)}, f32[128,1024]{1,0:T(8,128)S(1)}, u32[]{:S(2)}) copy-start(f32[128,1024]{1,0:T(8,128)S(1)} %times_columns.3) | copy-start | bytes 1572868
  165.3 16.5 %copy-start.32 = (f32[512]{0:T(512)}, f32[512]{0:T(512)S(1)}, u32[]{:S(2)}) copy-start(f32[512]{0:T(512)S(1)} %mul.338) | copy-start | bytes 6148
  168.8 26.8 %copy-start.26 = (f32[128,32]{0,1:T(8,128)}, f32[128,32]{0,1:T(8,128)S(1)}, u32[]{:S(2)}) copy-start(f32[128,32]{0,1:T(8,128)S(1)} %copy.143) | copy-start | bytes 49156
  169.7 12.1 %copy-start.55 = (f32[128]{0:T(128)}, f32[128]{0:T(128)S(1)}, u32[]{:S(2)}) copy-start(f32[128]{0:T(128)S(1)} %multiply_reduce_fusion.5) | copy-start | bytes 1540
  169.7 12.1 %copy-start.44 = (f32[128]{0:T(128)}, f32[128]{0:T(128)S(1)}, u32[]{:S(2)}) copy-start(f32[128]{0:T(128)S(1)} %fusion.58) | copy-start | bytes 1540
  212.5 426.5 %copy-start.5 = (f32[128,2048]{1,0:T(8,128)}, f32[128,2048]{1,0:T(8,128)S(1)}, u32[]{:S(2)}) copy-start(f32[128,2048]{1,0:T(8,128)S(1)} %get-tuple-element.68) | copy-start | bytes 3145732
  212.5 425.6 %copy-start.42 = (f32[128]{0:T(128)}, f32[128]{0:T(128)S(1)}, u32[]{:S(2)}) copy-start(f32[128]{0:T(128)S(1)} %fusion.59) | copy-start | bytes 1540
  440.6 10.2 %copy-start.60 = (bf16[4096,256]{1,0:T(8,128)(2,1)S(1)}, bf16[4096,256]{1,0:T(8,128)(2,1)}, u32[]{:S(2)}) copy-start(bf16[4096,256]{1,0:T(8,128)(2,1)} %get-tuple-element.47) | copy-start | bytes 6291460
  440.6 20.0 %slice-start.3 = ((s8[9437184]{0:T(1024)(128)(4,1)}), s8[4194304]{0:T(1024)(128)(4,1)S(1)}, s32[]{:S(2)}) async-start(s8[9437184]{0:T(1024)(128)(4,1)} %bitcast.201), calls=%async_computation.8 | async-start | bytes 8388608
  440.6 20.0 %slice-start.4 = ((s8[9437184]{0:T(1024)(128)(4,1)}), s8[4194304]{0:T(1024)(128)(4,1)S(1)}, s32[]{:S(2)}) async-start(s8[9437184]{0:T(1024)(128)(4,1)} %bitcast.201), calls=%async_computation.9 | async-start | bytes 8388608
  450.8 9.8 %slice-start.5 = ((s8[9437184]{0:T(1024)(128)(4,1)}), s8[1048576]{0:T(1024)(128)(4,1)S(1)}, s32[]{:S(2)}) async-start(s8[9437184]{0:T(1024)(128)(4,1)} %bitcast.201), calls=%async_computation.10 | async-start | bytes 2097152
  450.8 9.8 %copy-start.57 = (bf16[2304,704]{1,0:T(8,128)(2,1)S(1)}, bf16[2304,704]{1,0:T(8,128)(2,1)}, u32[]{:S(2)}) copy-start(bf16[2304,704]{1,0:T(8,128)(2,1)} %get-tuple-element.37) | copy-start | bytes 9732100
  450.8 18.7 %slice-start = ((s8[9437184]{0:T(1024)(128)(4,1)}), s8[4194304]{0:T(1024)(128)(4,1)S(1)}, s32[]{:S(2)}) async-start(s8[9437184]{0:T(1024)(128)(4,1)} %bitcast.199), calls=%async_computation.5 | async-start | bytes 8388608
  450.8 18.7 %slice-start.1 = ((s8[9437184]{0:T(1024)(128)(4,1)}), s8[4194304]{0:T(1024)(128)(4,1)S(1)}, s32[]{:S(2)}) async-start(s8[9437184]{0:T(1024)(128)(4,1)} %bitcast.199), calls=%async_computation.6 | async-start | bytes 8388608
  460.6 8.9 slice-start.2
  460.6 8.9 copy-start.59
  469.6 9.0 %copy-start.58 = (bf16[2304,704]{1,0:T(8,128)(2,1)S(1)}, bf16[2304,704]{1,0:T(8,128)(2,1)}, u32[]{:S(2)}) copy-start(bf16[2304,704]{1,0:T(8,128)(2,1)} %get-tuple-element.45) | copy-start | bytes 9732100
  632.6 239.4 %all-to-all-start.1 = ((bf16[32,64,256]{2,1,0:T(8,128)(2,1)}), bf16[32,64,256]{2,1,0:T(8,128)(2,1)}, u32[]{:S(2)}, u32[]{:S(2)}) async-start(bf16[32,64,256]{2,1,0:T(8,128)(2,1)} %bitcast.188), calls=%async_computation.2 | async-start | bytes 2097152 | tf_op jit(solution)/shard_map/all_to_all | solution.py:1203
  665.8 15.1 %copy-start.3 = (f32[128,1024]{1,0:T(8,128)S(1)}, f32[128,1024]{1,0:T(8,128)}, u32[]{:S(2)}) copy-start(f32[128,1024]{1,0:T(8,128)} %copy-done.2) | copy-start | bytes 1572868
  665.8 15.1 %copy-start.33 = (f32[512]{0:T(512)S(1)}, f32[512]{0:T(512)}, u32[]{:S(2)}) copy-start(f32[512]{0:T(512)} %copy-done.32) | copy-start | bytes 6148
  665.8 15.1 %copy-start.45 = (f32[128]{0:T(128)S(1)}, f32[128]{0:T(128)}, u32[]{:S(2)}) copy-start(f32[128]{0:T(128)} %copy-done.44) | copy-start | bytes 1540
  665.8 15.2 %copy-start.56 = (f32[128]{0:T(128)S(1)}, f32[128]{0:T(128)}, u32[]{:S(2)}) copy-start(f32[128]{0:T(128)} %copy-done.55) | copy-start | bytes 1540
  665.8 15.2 %copy-start.47 = (f32[32]{0:T(128)S(1)}, f32[32]{0:T(128)}, u32[]{:S(2)}) copy-start(f32[32]{0:T(128)} %copy-done.46) | copy-start | bytes 388
  665.8 15.2 %copy-start.49 = (f32[128]{0:T(128)S(1)}, f32[128]{0:T(128)}, u32[]{:S(2)}) copy-start(f32[128]{0:T(128)} %copy-done.48) | copy-start | bytes 1540
  666.7 14.8 %copy-start.15 = (bf16[16,128,256]{2,1,0:T(8,128)(2,1)S(1)}, bf16[16,128,256]{2,1,0:T(8,128)(2,1)}, u32[]{:S(2)}) copy-start(bf16[16,128,256]{2,1,0:T(8,128)(2,1)} %copy-done.14) | copy-start | bytes 3145732
  666.7 14.8 %copy-start.22 = (bf16[256,16,64]{0,2,1:T(8,128)(2,1)S(1)}, bf16[256,16,64]{0,2,1:T(8,128)(2,1)}, u32[]{:S(2)}) copy-start(bf16[256,16,64]{0,2,1:T(8,128)(2,1)} %broadcast_in_dim.110) | copy-start | bytes 1572868
  692.4 7.9 copy-start.1
  861.8 8.5 copy-start.54
  (39 other events, 145.2 us)
Sparse Core Ops, SparseCore 0:
  143.2 158.3 all-gather.1
  374.3 241.4 reduce-scatter.1

commit v3 on v2

--- a/solution.py
+++ b/solution.py
@@ -614,14 +614,14 @@
                 return carry
             lax.fori_loop(0, rows // 2, body, 0)
     one(0)
+    two(0)
     one(1)
-    two(0)
-    one(2)
     three(0)
     two(1)
-    one(3)
+    one(2)
     three(1)
     two(2)
+    one(3)
     three(2)
     two(3)
     three(3)
@@ -1055,6 +1055,7 @@
     )
     folded = jnp.concatenate(jnp.split(expand_proj, groups, axis=1), axis=0)
     aside = n_q + n_e + n_o + 5 * toks
+    wide = 6 * toks
     packed = jnp.concatenate(
         [
             query_proj,
@@ -1062,7 +1063,6 @@
             output_proj,
             jnp.pad(latent_proj, ((0, 0), (0, 5 * toks - n_l))),
             info,
-            jnp.zeros((rows, 2 * toks), bf),
         ],
         axis=1,
     )
@@ -1087,7 +1087,7 @@
 
     normed = norm_apply(inputs, gain_one).astype(bf)
     query_raw = times_columns(normed, weights, 0, n_q // 512, 512).reshape(toks, H, DN + DR)
-    latent_raw = times_columns(normed, weights, (n_q + n_e + n_o) // 512, 2, 512)[:, :n_l]
+    latent_raw = times_columns(normed, weights, (n_q + n_e + n_o) // wide, 1, wide)[:, :n_l]
     latent = latent_raw[:, :KVL]
     latent_normed = norm_apply(latent, gain_latent).astype(bf)
     positions = seq * toks + jnp.arange(toks, dtype=jnp.int32)
@@ -1239,14 +1239,14 @@
     d_pair = jnp.concatenate(
         [d_latent_pair, d_rotary_pair, jnp.zeros((2 * toks, 64), f32)], axis=1
     ).reshape(2, toks, -1)
-    d_pair = jnp.sum(seq_swap(d_pair, 8), axis=0)
+    d_pair = jnp.sum(seq_swap(d_pair.astype(bf), 8).astype(f32), axis=0)
     d_latent_normed = d_pair[:, :KVL]
     d_key_rotary = rotate(d_pair[:, KVL : KVL + DR], cosine, -sine)
     d_latent, latent_gain_grad = norm_back(latent, gain_latent, d_latent_normed)
     d_latent_raw = jnp.concatenate([d_latent, d_key_rotary], axis=1).astype(bf)
-    d_latent_wide = jnp.pad(d_latent_raw, ((0, 0), (0, 1024 - n_l)))
+    d_latent_wide = jnp.pad(d_latent_raw, ((0, 0), (0, wide - n_l)))
     d_normed = times_rows(d_query_raw, weights, 0, n_q, 512) + times_rows(
-        d_latent_wide, weights, (n_q + n_e + n_o) // 1024, 1024, 512
+        d_latent_wide, weights, (n_q + n_e + n_o) // wide, wide, 512
     )
     d_inputs, norm_gain_grad = norm_back(inputs, gain_one, d_normed)
     input_grad = d_middle + d_inputs
@@ -1262,7 +1262,6 @@
         ],
         axis=2,
     )
-    wide = 768
     gain_parts = jnp.pad(gain_parts, ((0, 0), (0, 0), (n_l, wide - n_l - 3))).astype(bf)
     grad_parts = packed_grads(
         n_dev,
@@ -1274,7 +1273,7 @@
         d_expanded,
         attended.T,
         d_attn,
-        d_latent_wide[:, :wide],
+        d_latent_wide,
         gain_parts,
     )
     grads = scatter_sum(grad_parts, 9)

time: 908 us -> 878 us (0.967)
  Pallas kernels: 716 us -> 697 us
    pallas_call x2, Pallas kernels: 279 us -> 270 us  [scatter_sum(): pl.pallas_call(functools.partial(rs_kernel, rows // 16), out_shape=jax.Sh...]
where the time goes in v3:
time: 878 us; the launch traced here: 868 us
  Pallas kernels  697 us (79%)
  local copies, waits for them, and re-layouts  60.5 us (7%)
  matrix products  58.1 us (7%)
  other arithmetic  26.7 us (3%)
  between operations  15.6 us (2%)
  starting transfers between devices  9.54 us (1%)
    pallas_call x2, Pallas kernels, scatter_sum(): pl.pallas_call(functools.partial(rs_kernel, rows // 16), out_shape=jax.Sh...  270 us
    pallas_call x2, Pallas kernels, gather_all(): pl.pallas_call(functools.partial(ag_kernel, rows // 16), out_shape=jax.Sh...  227 us
    pallas_call x2, Pallas kernels, by_tiles(): pl.pallas_call(kernel, grid=(steps,), out_shape=tuple((jax.ShapeDtypeStru...  119 us
    dot_general x5, matrix products, contract(): lax.dot_general(left, right, (((left_dim,), (right_dim,)), ((), ())), pre...  46.8 us
    pallas_call x1, Pallas kernels, packed_grads(): pl.pallas_call(functools.partial(grads_kernel, tile, n_q, n_e, n_o, fold)...  24.4 us
    pallas_call x3, Pallas kernels, times_rows(): pl.pallas_call(rows_kernel, grid=(k // tile,), out_shape=jax.ShapeDtypeSt...  17.6 us
  transfers between devices with their start and end apart: 4, of which 0 were waited for; matrix products, arithmetic and copies ran while one was open for 15% of the time, Pallas kernels for 66%

profile of v3, /device:TPU:0, one launch (start us, length us, event | category | flops | bytes accessed | tf_op | source)
XLA Modules:
  0.0 867.8 jit_solution(11012909561902170753)
XLA Ops:
  14.9 123.9 %gather_rows.2 = bf16[32,8,8,6912]{3,2,1,0:T(8,128)(2,1)} custom-call(bf16[8,8,6912]{2,1,0:T(8,128)(2,1)} %bitcast.181), custom_call_target="tpu_custom_call" | custom-call | bytes 457072000 | tf_op jit(solution)/shard_map/gather_rows/pallas_call | solution.py:501
  143.1 3.9 all-to-all-start
  150.1 2.5 times_columns.3
  152.6 7.3 times_columns.4
  163.5 8.2 seq_swap.2
  179.8 4.0 times_folded.1
  183.7 2.5 copy.165
  190.9 3.9 fusion.73
  196.3 2.9 convolution_convert_fusion.2
  200.5 5.1 times_columns.5
  207.0 103.6 %gather_rows.3 = bf16[32,16,8,2048]{3,2,1,0:T(8,128)(2,1)} custom-call(bf16[16,8,2048]{2,1,0:T(8,128)(2,1)} %fusion.28.x_ref), custom_call_target="tpu_custom_call" | custom-call | bytes 299376000 | tf_op jit(solution)/shard_map/gather_rows/pallas_call | solution.py:501
  312.1 54.9 %experts_forward.1 = (bf16[4096,2048]{1,0:T(8,128)(2,1)}, bf16[2304,2048]{1,0:T(8,128)(2,1)}, f32[2304,704]{1,0:T(8,128)}, f32[2304,704]{1,0:T(8,128)}, bf16[230...) custom-call(bf16[4096,2048]{1,0:T(8,128)(2,1)} %bitcast.152, ...), custom_call_target="tpu_custom_call" | custom-call | bytes 140000000 | tf_op jit(solution)/shard_map/experts_forward/pallas_call | solution.py:982
  368.3 64.0 %experts_backward.1 = (bf16[4096,2048]{1,0:T(8,128)(2,1)}, bf16[2304,2048]{1,0:T(8,128)(2,1)}, bf16[2304,704]{1,0:T(8,128)(2,1)}, bf16[2304,704]{1,0:T(8,128)(2,1)}, bf16[4096,256]{1,0:T(8,128)(2,1)}) custom-call(bf16[4096,2048]{1,0:T(8,128)(2,1)} %all-gather.2.cloned.1.call-done.c_ref, bf16[16,144,256]{2,1,0:T(8,128)(2,1)} %fusion.2.pick_ref, ...), custom_call_target="tpu_custom_call" | custom-call | bytes 175000000 | tf_op jit(solution)/shard_map/experts_backward/pallas_call | solution.py:982
  432.4 10.2 %fusion.19 = f32[88,2048]{1,0:T(8,128)} fusion(bf16[4096,2048]{1,0:T(8,128)(2,1)} %all-gather.2.cloned.1.call-done.c_ref, bf16[4096,128]{1,0:T(8,128)(2,1)} %get-tuple-element.46), kind=kOutput, calls=%fused_computation.45 | convolution fusion | flops 1476395008 | bytes 18546688 | tf_op jit(solution)/shard_map/dot_general | solution.py:49
  442.6 9.8 %convolution_convert_fusion = bf16[2048,256]{1,0:T(8,128)(2,1)} fusion(bf16[4096,2048]{1,0:T(8,128)(2,1)} %bitcast.153, bf16[4096,256]{1,0:T(8,128)(2,1)S(1)} %copy-done.45), kind=kOutput, calls=%fused_computation.2 | convolution fusion | flops 4295491584 | bytes 19922944 | tf_op jit(solution)/shard_map/dot_general | solution.py:49
  452.4 8.9 %fusion.74 = f32[704,2048]{1,0:T(8,128)} fusion(bf16[2304,704]{1,0:T(8,128)(2,1)S(1)} %copy-done.42, bf16[2304,2048]{1,0:T(8,128)(2,1)S(1)} %bitcast.202), kind=kOutput, calls=%fused_computation.168 | convolution fusion | flops 6643777536 | bytes 18448384 | tf_op jit(solution)/shard_map/dot_general | solution.py:49
  461.3 9.0 %fusion.75 = f32[2048,704]{0,1:T(8,128)} fusion(bf16[2304,2048]{1,0:T(8,128)(2,1)S(1)} %bitcast.200, bf16[2304,704]{1,0:T(8,128)(2,1)S(1)} %copy-done.44), kind=kOutput, calls=%fused_computation.169 | convolution fusion | flops 6643777536 | bytes 18448384 | tf_op jit(solution)/shard_map/dot_general | solution.py:49
  470.4 9.0 %fusion.76 = f32[2048,704]{0,1:T(8,128)} fusion(bf16[2304,2048]{1,0:T(8,128)(2,1)S(1)} %bitcast.200, bf16[2304,704]{1,0:T(8,128)(2,1)S(1)} %copy-done.43), kind=kOutput, calls=%fused_computation.170 | convolution fusion | flops 6643777536 | bytes 18448384 | tf_op jit(solution)/shard_map/dot_general | solution.py:49
  479.4 140.5 %scatter_sum.2 = f32[16,8,2048]{2,1,0:T(8,128)} custom-call(bf16[32,16,8,2048]{3,2,1,0:T(8,128)(2,1)} %bitcast.154), custom_call_target="tpu_custom_call" | custom-call | bytes 299376000 | tf_op jit(solution)/shard_map/scatter_sum/pallas_call | solution.py:649
  621.6 5.6 all-to-all-start.1
  627.6 6.1 times_rows.3
  635.5 2.8 multiply_reduce_fusion
  646.5 2.9 copy.164.x_ref.dexp_ref
  651.6 4.3 times_folded_back.1
  656.9 8.0 seq_swap.3
  668.1 7.8 times_rows.4
  676.2 3.7 times_rows.5
  683.2 24.4 %packed_grads.1 = bf16[32,64,6912]{2,1,0:T(8,128)(2,1)} custom-call(bf16[2048,128]{1,0:T(8,128)(2,1)} %copy.159.normed_ref, bf16[128,3072]{1,0:T(8,128)(2,1)} %copy-done.1, bf16[512,256]{1,0:T(8,128)(2,1)} %get-tuple-element.87.full_ref, bf16[256,4096]{1,0:T(8,128)(2,1)} %copy-done, bf16[2048,128]{1,0:T(8,128)(2,1)} %bitcast.180, ...), custom_call_target="tpu_custom_call" | custom-call | tf_op jit(solution)/shard_map/packed_grads/pallas_call | solution.py:898
  707.6 129.0 %scatter_sum.3 = f32[8,8,6912]{2,1,0:T(8,128)} custom-call(bf16[32,8,8,6912]{3,2,1,0:T(8,128)(2,1)} %bitcast.151), custom_call_target="tpu_custom_call" | custom-call | bytes 457072000 | tf_op jit(solution)/shard_map/scatter_sum/pallas_call | solution.py:649
  851.5 2.9 copy.161
  854.4 2.7 reshape.435
  857.0 3.5 fusion.14
  (238 shorter events, 74.6 us)
Async XLA Ops:
  7.2 361.1 %all-gather.2.cloned.1.call-start = ((), (), s32[]{:S(2)}) async-start(), calls=%async_computation.4 | async-start | bytes 17301504 | tf_op jit(solution)/shard_map/all_gather | solution.py:1086
  14.9 123.9 %copy-start.24 = (bf16[64,2816]{1,0:T(8,128)(2,1)S(1)}, bf16[64,2816]{1,0:T(8,128)(2,1)}, u32[]{:S(2)}) copy-start(bf16[64,2816]{1,0:T(8,128)(2,1)} %param.26) | copy-start | bytes 1081348
  143.1 169.1 %all-to-all-start = ((bf16[32,64,256]{2,1,0:T(8,128)(2,1)}), bf16[32,64,256]{2,1,0:T(8,128)(2,1)}, u32[]{:S(2)}, u32[]{:S(2)}) async-start(bf16[32,64,256]{2,1,0:T(8,128)(2,1)} %fusion.16), calls=%async_computation | async-start | bytes 2097152 | tf_op jit(solution)/shard_map/all_to_all | solution.py:1082
  147.0 710.1 %reduce-scatter.2.cloned.1.call-start = ((), (), s32[]{:S(2)}) async-start(), calls=%async_computation.3 | async-start | bytes 17301504 | tf_op jit(solution)/shard_map/reduce_scatter | solution.py:1166
  152.6 9.9 %copy-start.2 = (f32[128,768]{1,0:T(8,128)}, f32[128,768]{1,0:T(8,128)S(1)}, u32[]{:S(2)}) copy-start(f32[128,768]{1,0:T(8,128)S(1)} %times_columns.3) | copy-start | bytes 1179652
  152.6 7.3 copy-start.37
  161.8 13.3 %copy-start.35 = (f32[128]{0:T(128)}, f32[128]{0:T(128)S(1)}, u32[]{:S(2)}) copy-start(f32[128]{0:T(128)S(1)} %get-tuple-element.103) | copy-start | bytes 1540
  162.3 12.7 %copy-start.29 = (bf16[640]{0:T(1024)(128)(2,1)}, bf16[640]{0:T(1024)(128)(2,1)S(1)}, u32[]{:S(2)}) copy-start(bf16[640]{0:T(1024)(128)(2,1)S(1)} %pad.80.clone) | copy-start | bytes 3844
  162.5 12.6 %copy-start.40 = (f32[128]{0:T(128)}, f32[128]{0:T(128)S(1)}, u32[]{:S(2)}) copy-start(f32[128]{0:T(128)S(1)} %multiply_reduce_fusion.5) | copy-start | bytes 1540
  162.5 12.6 %copy-start.31 = (f32[128]{0:T(128)}, f32[128]{0:T(128)S(1)}, u32[]{:S(2)}) copy-start(f32[128]{0:T(128)S(1)} %fusion.58) | copy-start | bytes 1540
  205.8 421.4 %copy-start.6 = (f32[128,2048]{1,0:T(8,128)}, f32[128,2048]{1,0:T(8,128)S(1)}, u32[]{:S(2)}) copy-start(f32[128,2048]{1,0:T(8,128)S(1)} %get-tuple-element.68) | copy-start | bytes 3145732
  432.4 10.2 %copy-start.45 = (bf16[4096,256]{1,0:T(8,128)(2,1)S(1)}, bf16[4096,256]{1,0:T(8,128)(2,1)}, u32[]{:S(2)}) copy-start(bf16[4096,256]{1,0:T(8,128)(2,1)} %get-tuple-element.47) | copy-start | bytes 6291460
  432.4 20.0 %slice-start.3 = ((s8[9437184]{0:T(1024)(128)(4,1)}), s8[4194304]{0:T(1024)(128)(4,1)S(1)}, s32[]{:S(2)}) async-start(s8[9437184]{0:T(1024)(128)(4,1)} %bitcast.201), calls=%async_computation.8 | async-start | bytes 8388608
  432.4 20.0 %slice-start.4 = ((s8[9437184]{0:T(1024)(128)(4,1)}), s8[4194304]{0:T(1024)(128)(4,1)S(1)}, s32[]{:S(2)}) async-start(s8[9437184]{0:T(1024)(128)(4,1)} %bitcast.201), calls=%async_computation.9 | async-start | bytes 8388608
  442.6 9.8 %slice-start.5 = ((s8[9437184]{0:T(1024)(128)(4,1)}), s8[1048576]{0:T(1024)(128)(4,1)S(1)}, s32[]{:S(2)}) async-start(s8[9437184]{0:T(1024)(128)(4,1)} %bitcast.201), calls=%async_computation.10 | async-start | bytes 2097152
  442.6 9.8 %copy-start.42 = (bf16[2304,704]{1,0:T(8,128)(2,1)S(1)}, bf16[2304,704]{1,0:T(8,128)(2,1)}, u32[]{:S(2)}) copy-start(bf16[2304,704]{1,0:T(8,128)(2,1)} %get-tuple-element.37) | copy-start | bytes 9732100
  442.6 18.7 %slice-start = ((s8[9437184]{0:T(1024)(128)(4,1)}), s8[4194304]{0:T(1024)(128)(4,1)S(1)}, s32[]{:S(2)}) async-start(s8[9437184]{0:T(1024)(128)(4,1)} %bitcast.199), calls=%async_computation.5 | async-start | bytes 8388608
  442.6 18.7 %slice-start.1 = ((s8[9437184]{0:T(1024)(128)(4,1)}), s8[4194304]{0:T(1024)(128)(4,1)S(1)}, s32[]{:S(2)}) async-start(s8[9437184]{0:T(1024)(128)(4,1)} %bitcast.199), calls=%async_computation.6 | async-start | bytes 8388608
  452.4 8.9 %slice-start.2 = ((s8[9437184]{0:T(1024)(128)(4,1)}), s8[1048576]{0:T(1024)(128)(4,1)S(1)}, s32[]{:S(2)}) async-start(s8[9437184]{0:T(1024)(128)(4,1)} %bitcast.199), calls=%async_computation.7 | async-start | bytes 2097152
  452.4 8.9 %copy-start.44 = (bf16[2304,704]{1,0:T(8,128)(2,1)S(1)}, bf16[2304,704]{1,0:T(8,128)(2,1)}, u32[]{:S(2)}) copy-start(bf16[2304,704]{1,0:T(8,128)(2,1)} %get-tuple-element.44) | copy-start | bytes 9732100
  461.3 9.0 %copy-start.43 = (bf16[2304,704]{1,0:T(8,128)(2,1)S(1)}, bf16[2304,704]{1,0:T(8,128)(2,1)}, u32[]{:S(2)}) copy-start(bf16[2304,704]{1,0:T(8,128)(2,1)} %get-tuple-element.45) | copy-start | bytes 9732100
  619.9 7.3 copy-start.10
  621.6 225.2 %all-to-all-start.1 = ((bf16[32,64,256]{2,1,0:T(8,128)(2,1)}), bf16[32,64,256]{2,1,0:T(8,128)(2,1)}, u32[]{:S(2)}, u32[]{:S(2)}) async-start(bf16[32,64,256]{2,1,0:T(8,128)(2,1)} %bitcast.188), calls=%async_computation.2 | async-start | bytes 2097152 | tf_op jit(solution)/shard_map/all_to_all | solution.py:1203
  656.0 10.0 %copy-start.3 = (f32[128,768]{1,0:T(8,128)S(1)}, f32[128,768]{1,0:T(8,128)}, u32[]{:S(2)}) copy-start(f32[128,768]{1,0:T(8,128)} %copy-done.2) | copy-start | bytes 1179652
  656.0 10.0 %copy-start.28 = (f32[512]{0:T(512)S(1)}, f32[512]{0:T(512)}, u32[]{:S(2)}) copy-start(f32[512]{0:T(512)} %copy-done.27) | copy-start | bytes 6148
  656.0 10.0 %copy-start.32 = (f32[128]{0:T(128)S(1)}, f32[128]{0:T(128)}, u32[]{:S(2)}) copy-start(f32[128]{0:T(128)} %copy-done.31) | copy-start | bytes 1540
  656.0 10.2 %copy-start.34 = (f32[32]{0:T(128)S(1)}, f32[32]{0:T(128)}, u32[]{:S(2)}) copy-start(f32[32]{0:T(128)} %copy-done.33) | copy-start | bytes 388
  656.0 10.2 %copy-start.36 = (f32[128]{0:T(128)S(1)}, f32[128]{0:T(128)}, u32[]{:S(2)}) copy-start(f32[128]{0:T(128)} %copy-done.35) | copy-start | bytes 1540
  656.1 10.6 %copy-start.41 = (f32[128]{0:T(128)S(1)}, f32[128]{0:T(128)}, u32[]{:S(2)}) copy-start(f32[128]{0:T(128)} %copy-done.40) | copy-start | bytes 1540
  656.1 11.7 %copy-start.16 = (bf16[128,16,128]{0,2,1:T(8,128)(2,1)S(1)}, bf16[128,16,128]{0,2,1:T(8,128)(2,1)}, u32[]{:S(2)}) copy-start(bf16[128,16,128]{0,2,1:T(8,128)(2,1)} %slice.237) | copy-start | bytes 1572868
  668.1 7.9 copy-start.1
  836.6 8.5 copy-start.39
  (24 other events, 72.9 us)
Sparse Core Ops, SparseCore 0:
  139.0 155.1 all-gather.1
  367.2 242.8 reduce-scatter.1
